TPU v7x, 512 devices: a whole 4x8x8 slice. The times are simulated.
512 devices in a mesh: seq: 128 (over y, z, x_lo), mp: 2 (over x_hi), batch: 2 (over core).
Axes of the slice: x: 4 (x_hi: 2, x_lo: 2; x = x_hi * 2 + x_lo), y: 8, z: 8, core: 2. Of those that a mesh axis runs over, the one named last changes fastest.
Arguments:
- queries: bfloat16 [256, 256, 512], P(('batch', 'seq'), None, 'mp'), parts along dimension 0, may hold values from -10 to 10
- key_vectors: bfloat16 [256, 256, 512], P(('batch', 'seq'), None, 'mp'), parts along dimension 0, may hold values from -10 to 10
- value_vectors: bfloat16 [256, 256, 512], P(('batch', 'seq'), None, 'mp'), parts along dimension 0, may hold values from -6 to 6
- cotangent: bfloat16 [256, 256, 512], P(('batch', 'seq'), None, 'mp'), parts along dimension 0, may hold values from -6 to 6
- row_pattern: int32 [4, 2, 2], P('mp'), may hold values from 0 to 1, as said below
- column_pattern: int32 [4, 4, 4], P('mp'), may hold values from 0 to 1, as said below
Outputs:
- attended: bfloat16 [256, 256, 512], P(('batch', 'seq'), None, 'mp'), parts along dimension 0
- grad_queries: bfloat16 [256, 256, 512], P(('batch', 'seq'), None, 'mp'), parts along dimension 0
- grad_keys: bfloat16 [256, 256, 512], P(('batch', 'seq'), None, 'mp'), parts along dimension 0
- grad_values: bfloat16 [256, 256, 512], P(('batch', 'seq'), None, 'mp'), parts along dimension 0
There are 2 independent parts, one for each index of `batch`. A program takes and returns all parts, laid end to end along the dimension named above; an argument that names none is the same for every part. Nothing has to cross between parts.
Inputs may be any that keep to these rules, and one draw needn't show every extreme that they name: `row_pattern`: every diagonal entry is 1. `column_pattern`: every diagonal entry is 1 and every entry above the diagonal is 0.
All inputs are finite; a program needn't handle non-finite values.
Results may differ from a plain program's by a relative error of at most 0.04.
Values may be sent and summed in bfloat16 or wider, within the bound.
A program may use at most 64 MiB of HBM per device.

v0:
```python
import math

import jax
import jax.numpy as jnp
from jax import lax
from jax.sharding import PartitionSpec as P

DH = 64
CBLK = 128
RB = 4


NEG = -1e30


def passed_along(block, axis, distance):
    devices = range(lax.axis_size(axis))
    route = [(i - distance, i) for i in devices if i - distance in devices]
    return lax.ppermute(block, axis, route)


def for_sending(x):
    return jax.tree.map(lambda a: a.astype(jnp.bfloat16) if a.dtype == jnp.float32 else a, x)


def product(formula, left, right):
    return jnp.einsum(formula, left, right, preferred_element_type=jnp.float32)


def expand(pattern, block):
    return jnp.repeat(jnp.repeat(pattern, block, axis=1), block, axis=2) > 0


def masked_scores(queries, key_block, allowed, layout):
    key_layout = layout.replace("q", "k")
    scaling = 1.0 / math.sqrt(queries.shape[-1])
    scores = product(layout + "," + key_layout + "->bhqk", queries, key_block) * scaling
    return jnp.where(allowed, scores, NEG)


def attend(queries, key_block, value_block, allowed, layout):
    key_layout = layout.replace("q", "k")
    scores = masked_scores(queries, key_block, allowed, layout)
    highest = jnp.max(scores, axis=-1)
    log_total = highest + jnp.log(jnp.sum(jnp.exp(scores - highest[..., None]), axis=-1))
    weights = jnp.exp(scores - log_total[..., None]).astype(jnp.bfloat16)
    attended = product("bhqk," + key_layout + "->" + layout, weights, value_block).astype(
        jnp.bfloat16
    )
    return (attended, log_total)


def row_dots(grads, attended, layout):
    return product(layout + "," + layout + "->bhq", grads, attended)


def backprop(queries, key_block, value_block, grads, log_total, dots, allowed, layout):
    key_layout = layout.replace("q", "k")
    scaling = 1.0 / math.sqrt(queries.shape[-1])
    scores = masked_scores(queries, key_block, allowed, layout)
    weights = jnp.exp(scores - log_total[..., None])
    rounded = weights.astype(jnp.bfloat16)
    weight_grads = product(layout + "," + key_layout + "->bhqk", grads, value_block)
    score_grads = (weights * (weight_grads - dots[..., None])).astype(jnp.bfloat16)
    grad_query = product("bhqk," + key_layout + "->" + layout, score_grads, key_block) * scaling
    grad_key = product("bhqk," + layout + "->" + key_layout, score_grads, queries) * scaling
    grad_value = product("bhqk," + layout + "->" + key_layout, rounded, grads)
    return (grad_query, grad_key, grad_value)


def per_device(queries, key_vectors, value_vectors, cotangent, row_pattern, column_pattern):
    local_rows, width, features = queries.shape
    half_width = features // 2
    heads_half = half_width // DH
    head_shape = (local_rows, width, heads_half, DH)
    row_queries = queries[:, :, :half_width].reshape(head_shape)
    row_keys = key_vectors[:, :, :half_width].reshape(head_shape)
    row_values = value_vectors[:, :, :half_width].reshape(head_shape)
    row_grads = cotangent[:, :, :half_width].reshape(head_shape)
    received = passed_along(
        (key_vectors[-1:, :, :half_width], value_vectors[-1:, :, :half_width]), "seq", 1
    )
    one_shape = (1, width, heads_half, DH)
    earlier_keys = jnp.concatenate([received[0].reshape(one_shape), row_keys[:-1]], axis=0)
    earlier_values = jnp.concatenate([received[1].reshape(one_shape), row_values[:-1]], axis=0)
    key_block = jnp.concatenate([earlier_keys, row_keys], axis=1)
    value_block = jnp.concatenate([earlier_values, row_values], axis=1)
    block_map = expand(row_pattern, CBLK)
    column_ids = jnp.arange(width, dtype=jnp.int32)
    same_row = block_map & (column_ids[None, None, :] <= column_ids[None, :, None])
    earlier_row = block_map & (column_ids[None, None, :] > column_ids[None, :, None])
    global_rows = lax.axis_index("seq") * local_rows + jnp.arange(local_rows, dtype=jnp.int32)

    def row_pass(members):
        query_row, keys_here, values_here, grads_here, row_number = members
        allowed = jnp.concatenate([earlier_row & (row_number >= 1), same_row], axis=-1)[None]
        attended_row, total_row = attend(
            query_row[None], keys_here[None], values_here[None], allowed, "bqhd"
        )
        dot_row = row_dots(grads_here[None], attended_row, "bqhd")
        dq_row, dk_row, dv_row = backprop(
            query_row[None],
            keys_here[None],
            values_here[None],
            grads_here[None],
            total_row,
            dot_row,
            allowed,
            "bqhd",
        )
        return (attended_row[0], total_row[0], dot_row[0], dq_row[0], dk_row[0], dv_row[0])

    row_attended, row_total, row_dot, grad_query, key_cat, value_cat = lax.map(
        row_pass, (row_queries, key_block, value_block, row_grads, global_rows)
    )
    column_queries = queries[:, :, half_width:]
    column_keys = key_vectors[:, :, half_width:]
    column_values = value_vectors[:, :, half_width:]
    column_grads = cotangent[:, :, half_width:]
    moved_q, moved_k, moved_v = (
        lax.all_to_all(column_queries, "seq", split_axis=1, concat_axis=0, tiled=True),
        lax.all_to_all(column_keys, "seq", split_axis=1, concat_axis=0, tiled=True),
        lax.all_to_all(column_values, "seq", split_axis=1, concat_axis=0, tiled=True),
    )
    all_rows, few_columns = (moved_q.shape[0], moved_q.shape[1])
    column_shape = (all_rows, few_columns, heads_half, DH)
    column_block = expand(column_pattern, all_rows // RB)
    row_ids = jnp.arange(all_rows, dtype=jnp.int32)
    column_allowed = (column_block & (row_ids[None, None, :] <= row_ids[None, :, None]))[None]
    stacked_q = moved_q.reshape(column_shape)
    stacked_k = moved_k.reshape(column_shape)
    stacked_v = moved_v.reshape(column_shape)
    column_attended, column_total = attend(stacked_q, stacked_k, stacked_v, column_allowed, "qbhd")
    incoming = passed_along(
        (
            for_sending(key_cat[:1, :width].reshape(1, width, half_width)),
            for_sending(value_cat[:1, :width].reshape(1, width, half_width)),
        ),
        "seq",
        -1,
    )
    tail_keys = incoming[0].reshape(one_shape)
    tail_values = incoming[1].reshape(one_shape)
    grad_key = key_cat[:, width:] + jnp.concatenate([key_cat[1:, :width], tail_keys], axis=0)
    grad_value = value_cat[:, width:] + jnp.concatenate(
        [value_cat[1:, :width], tail_values], axis=0
    )
    moved_g = lax.all_to_all(column_grads, "seq", split_axis=1, concat_axis=0, tiled=True)
    stacked_g = moved_g.reshape(column_shape)
    column_dot = row_dots(stacked_g, column_attended, "qbhd")
    column_dq, column_dk, column_dv = backprop(
        stacked_q, stacked_k, stacked_v, stacked_g, column_total, column_dot, column_allowed, "qbhd"
    )
    flat_shape = (all_rows, few_columns, half_width)
    returned = (
        lax.all_to_all(
            column_attended.reshape(flat_shape), "seq", split_axis=0, concat_axis=1, tiled=True
        ),
        lax.all_to_all(
            column_dq.astype(jnp.bfloat16).reshape(flat_shape),
            "seq",
            split_axis=0,
            concat_axis=1,
            tiled=True,
        ),
        lax.all_to_all(
            column_dk.astype(jnp.bfloat16).reshape(flat_shape),
            "seq",
            split_axis=0,
            concat_axis=1,
            tiled=True,
        ),
        lax.all_to_all(
            column_dv.astype(jnp.bfloat16).reshape(flat_shape),
            "seq",
            split_axis=0,
            concat_axis=1,
            tiled=True,
        ),
    )
    row_flat = (local_rows, width, half_width)
    attended = jnp.concatenate([row_attended.reshape(row_flat), returned[0]], axis=2)
    grad_queries = jnp.concatenate(
        [grad_query.astype(jnp.bfloat16).reshape(row_flat), returned[1]], axis=2
    )
    grad_keys = jnp.concatenate(
        [grad_key.astype(jnp.bfloat16).reshape(row_flat), returned[2]], axis=2
    )
    grad_values = jnp.concatenate(
        [grad_value.astype(jnp.bfloat16).reshape(row_flat), returned[3]], axis=2
    )
    return (attended, grad_queries, grad_keys, grad_values)


def solution(mesh):
    placed = (
        P(("batch", "seq"), None, "mp"),
        P(("batch", "seq"), None, "mp"),
        P(("batch", "seq"), None, "mp"),
        P(("batch", "seq"), None, "mp"),
        P("mp", None, None),
        P("mp", None, None),
    )
    return jax.shard_map(
        per_device,
        mesh=mesh,
        in_specs=placed,
        out_specs=(
            P(("batch", "seq"), None, "mp"),
            P(("batch", "seq"), None, "mp"),
            P(("batch", "seq"), None, "mp"),
            P(("batch", "seq"), None, "mp"),
        ),
        check_vma=False,
    )
```

profile of v0, /device:TPU:4, one launch (start us, length us, event | category | flops | bytes accessed | tf_op | source)
XLA Modules:
  0.0 174.9 jit_solution(3886166148914717893)
XLA Ops:
  0.6 0.9 fusion.29
  1.6 0.6 copy.142
  2.3 18.4 %all-to-all-start = ((bf16[128,2,128]{2,1,0:T(2,128)(2,1)}), bf16[128,2,128]{2,1,0:T(2,128)(2,1)S(1)}, u32[]{:S(2)}, u32[]{:S(2)}) async-start(bf16[128,2,128]{2,1,0:T(2,128)(2,1)} %bitcast.134), calls=%async_computation | async-start | bytes 131072 | tf_op jit(solution)/shard_map/all_to_all | solution.py:121
  20.8 3.2 %collective-permute-start.1 = (bf16[1,256,128]{2,1,0:T(8,128)(2,1)S(1)}, bf16[1,256,128]{2,1,0:T(8,128)(2,1)S(1)}, u32[]{:S(2)}, u32[]{:S(2)}) collective-permute-start(bf16[1,256,128]{2,1,0:T(8,128)(2,1)S(1)} %get-tuple-element.32), channel_id=1, source_target_pairs={{0,4},{4,8},{8,12},{12,16},{16,20},{20,24},{24,28},{28,32},{32,36}... | collective-permute-start | bytes 196616 | tf_op jit(solution)/shard_map/ppermute | solution.py:19
  24.0 3.4 %collective-permute-start = (bf16[1,256,128]{2,1,0:T(8,128)(2,1)S(1)}, bf16[1,256,128]{2,1,0:T(8,128)(2,1)S(1)}, u32[]{:S(2)}, u32[]{:S(2)}) collective-permute-start(bf16[1,256,128]{2,1,0:T(8,128)(2,1)S(1)} %get-tuple-element.30), channel_id=1, source_target_pairs={{0,4},{4,8},{8,12},{12,16},{16,20},{20,24},{24,28},{28,32},{32,36}... | collective-permute-start | bytes 196616 | tf_op jit(solution)/shard_map/ppermute | solution.py:19
  27.4 0.1 copy.72
  27.5 0.1 copy.69
  27.6 0.7 copy-done.4
  28.3 0.1 copy.70
  28.5 0.5 copy-done.3
  29.0 0.1 copy.75
  29.3 0.1 copy.73
  29.5 0.6 copy.143
  30.3 0.6 copy.141
  30.9 0.3 copy-done.2
  31.4 0.6 copy.144
  32.1 0.1 fusion.13
  32.4 0.4 fusion.31
  32.8 0.2 exponential_reduce_fusion
  33.1 0.3 fusion.19
  33.4 0.4 fusion.4
  33.8 0.2 fusion.9
  34.0 14.1 %all-to-all-start.1 = ((bf16[128,2,128]{2,1,0:T(2,128)(2,1)}), bf16[128,2,128]{2,1,0:T(2,128)(2,1)S(1)}, u32[]{:S(2)}, u32[]{:S(2)}) async-start(bf16[128,2,128]{2,1,0:T(2,128)(2,1)} %bitcast.135), calls=%async_computation.1 | async-start | bytes 131072 | tf_op jit(solution)/shard_map/all_to_all | solution.py:122
  48.1 0.3 convolution_bitcast_fusion
  48.4 11.6 %all-to-all-done.1 = bf16[128,2,128]{2,1,0:T(2,128)(2,1)S(1)} async-done(((bf16[128,2,128]{2,1,0:T(2,128)(2,1)}), bf16[128,2,128]{2,1,0:T(2,128)(2,1)S(1)}, u32[]{:S(2)}, u32[]{:S(2)}) %all-to-all-start.1) | async-done | bytes 65568 | tf_op jit(solution)/shard_map/all_to_all | solution.py:122
  60.0 6.1 %all-to-all-start.2 = ((bf16[128,2,128]{2,1,0:T(2,128)(2,1)}), bf16[128,2,128]{2,1,0:T(2,128)(2,1)S(1)}, u32[]{:S(2)}, u32[]{:S(2)}) async-start(bf16[128,2,128]{2,1,0:T(2,128)(2,1)} %bitcast.133), calls=%async_computation.2 | async-start | bytes 131072 | tf_op jit(solution)/shard_map/all_to_all | solution.py:123
  66.2 0.3 fusion.5
  66.5 0.1 copy.84
  66.6 0.1 copy.94
  66.7 1.3 collective-permute-start.3
  68.0 1.3 collective-permute-start.2
  69.4 0.4 bitcast_reduce_fusion.2
  69.8 8.3 %all-to-all-done.2 = bf16[128,2,128]{2,1,0:T(2,128)(2,1)S(1)} async-done(((bf16[128,2,128]{2,1,0:T(2,128)(2,1)}), bf16[128,2,128]{2,1,0:T(2,128)(2,1)S(1)}, u32[]{:S(2)}, u32[]{:S(2)}) %all-to-all-start.2) | async-done | bytes 65568 | tf_op jit(solution)/shard_map/all_to_all | solution.py:123
  78.1 9.8 %all-to-all-start.4 = ((bf16[128,2,128]{2,1,0:T(2,128)(2,1)}), bf16[128,2,128]{2,1,0:T(2,128)(2,1)S(1)}, u32[]{:S(2)}, u32[]{:S(2)}) async-start(bf16[128,2,128]{2,1,0:T(2,128)(2,1)} %bitcast.136), calls=%async_computation.4 | async-start | bytes 131072 | tf_op jit(solution)/shard_map/all_to_all | solution.py:148
  87.9 0.4 bitcast_reduce_fusion.1
  88.7 0.4 bitcast_reduce_fusion.3
  89.3 10.3 %all-to-all-done.4 = bf16[128,2,128]{2,1,0:T(2,128)(2,1)S(1)} async-done(((bf16[128,2,128]{2,1,0:T(2,128)(2,1)}), bf16[128,2,128]{2,1,0:T(2,128)(2,1)S(1)}, u32[]{:S(2)}, u32[]{:S(2)}) %all-to-all-start.4) | async-done | bytes 65568 | tf_op jit(solution)/shard_map/all_to_all | solution.py:148
  99.6 0.4 bitcast_reduce_fusion
  100.2 0.3 fusion.30
  100.6 0.2 convolution_convert_fusion.1
  100.7 0.2 copy.120
  100.9 0.8 copy.83
  101.7 6.1 %all-to-all-start.3 = ((bf16[128,2,128]{2,1,0:T(2,128)(2,1)}), bf16[128,2,128]{2,1,0:T(2,128)(2,1)S(1)}, u32[]{:S(2)}, u32[]{:S(2)}) async-start(bf16[128,2,128]{2,1,0:T(2,128)(2,1)} %copy.83), calls=%async_computation.3 | async-start | bytes 131072 | tf_op jit(solution)/shard_map/all_to_all | solution.py:156
  107.9 0.2 convolution_convert_fusion.2
  108.1 0.5 multiply_reduce_fusion
  108.6 0.3 fusion.8
  108.9 0.2 fusion.10
  109.1 0.2 fusion.11
  109.3 0.8 copy.103
  110.0 0.8 copy.93
  110.8 0.7 copy.98
  111.5 8.2 %all-to-all-done.3 = bf16[128,2,128]{2,1,0:T(2,128)(2,1)S(1)} async-done(((bf16[128,2,128]{2,1,0:T(2,128)(2,1)}), bf16[128,2,128]{2,1,0:T(2,128)(2,1)S(1)}, u32[]{:S(2)}, u32[]{:S(2)}) %all-to-all-start.3) | async-done | bytes 65568 | tf_op jit(solution)/shard_map/all_to_all | solution.py:156
  119.8 6.4 %all-to-all-start.7 = ((bf16[128,2,128]{2,1,0:T(2,128)(2,1)}), bf16[128,2,128]{2,1,0:T(2,128)(2,1)S(1)}, u32[]{:S(2)}, u32[]{:S(2)}) async-start(bf16[128,2,128]{2,1,0:T(2,128)(2,1)} %copy.103), calls=%async_computation.7 | async-start | bytes 131072 | tf_op jit(solution)/shard_map/all_to_all | solution.py:173
  126.2 11.9 %all-to-all-done.7 = bf16[128,2,128]{2,1,0:T(2,128)(2,1)S(1)} async-done(((bf16[128,2,128]{2,1,0:T(2,128)(2,1)}), bf16[128,2,128]{2,1,0:T(2,128)(2,1)S(1)}, u32[]{:S(2)}, u32[]{:S(2)}) %all-to-all-start.7) | async-done | bytes 65568 | tf_op jit(solution)/shard_map/all_to_all | solution.py:173
  138.1 6.1 %all-to-all-start.5 = ((bf16[128,2,128]{2,1,0:T(2,128)(2,1)}), bf16[128,2,128]{2,1,0:T(2,128)(2,1)S(1)}, u32[]{:S(2)}, u32[]{:S(2)}) async-start(bf16[128,2,128]{2,1,0:T(2,128)(2,1)} %copy.93), calls=%async_computation.5 | async-start | bytes 131072 | tf_op jit(solution)/shard_map/all_to_all | solution.py:159
  144.3 0.1 copy.104
  144.4 0.1 copy.99
  144.5 0.7 pad_maximum_fusion
  145.2 11.0 %all-to-all-done.5 = bf16[128,2,128]{2,1,0:T(2,128)(2,1)S(1)} async-done(((bf16[128,2,128]{2,1,0:T(2,128)(2,1)}), bf16[128,2,128]{2,1,0:T(2,128)(2,1)S(1)}, u32[]{:S(2)}, u32[]{:S(2)}) %all-to-all-start.5) | async-done | bytes 65568 | tf_op jit(solution)/shard_map/all_to_all | solution.py:159
  156.1 6.1 %all-to-all-start.6 = ((bf16[128,2,128]{2,1,0:T(2,128)(2,1)}), bf16[128,2,128]{2,1,0:T(2,128)(2,1)S(1)}, u32[]{:S(2)}, u32[]{:S(2)}) async-start(bf16[128,2,128]{2,1,0:T(2,128)(2,1)} %copy.98), calls=%async_computation.6 | async-start | bytes 131072 | tf_op jit(solution)/shard_map/all_to_all | solution.py:166
  162.2 0.7 pad_maximum_fusion.1
  162.9 0.7 pad_maximum_fusion.3
  163.6 10.6 %all-to-all-done.6 = bf16[128,2,128]{2,1,0:T(2,128)(2,1)S(1)} async-done(((bf16[128,2,128]{2,1,0:T(2,128)(2,1)}), bf16[128,2,128]{2,1,0:T(2,128)(2,1)S(1)}, u32[]{:S(2)}, u32[]{:S(2)}) %all-to-all-start.6) | async-done | bytes 65568 | tf_op jit(solution)/shard_map/all_to_all | solution.py:166
  174.2 0.7 pad_maximum_fusion.2
  (51 shorter events, 2.3 us)
Async XLA Ops:
  1.6 19.1 %copy-start = (bf16[1,256,256]{2,1,0:T(8,128)(2,1)S(1)}, bf16[1,256,256]{2,1,0:T(8,128)(2,1)}, u32[]{:S(2)}) copy-start(bf16[1,256,256]{2,1,0:T(8,128)(2,1)} %param.7) | copy-start | bytes 393220
  2.3 31.7 %all-to-all-start = ((bf16[128,2,128]{2,1,0:T(2,128)(2,1)}), bf16[128,2,128]{2,1,0:T(2,128)(2,1)S(1)}, u32[]{:S(2)}, u32[]{:S(2)}) async-start(bf16[128,2,128]{2,1,0:T(2,128)(2,1)} %bitcast.134), calls=%async_computation | async-start | bytes 131072 | tf_op jit(solution)/shard_map/all_to_all | solution.py:121
  20.7 3.2 %copy-start.1 = (bf16[1,256,256]{2,1,0:T(8,128)(2,1)S(1)}, bf16[1,256,256]{2,1,0:T(8,128)(2,1)}, u32[]{:S(2)}) copy-start(bf16[1,256,256]{2,1,0:T(8,128)(2,1)} %param.8) | copy-start | bytes 393220
  20.8 11.5 %collective-permute-start.1 = (bf16[1,256,128]{2,1,0:T(8,128)(2,1)S(1)}, bf16[1,256,128]{2,1,0:T(8,128)(2,1)S(1)}, u32[]{:S(2)}, u32[]{:S(2)}) collective-permute-start(bf16[1,256,128]{2,1,0:T(8,128)(2,1)S(1)} %get-tuple-element.32), channel_id=1, source_target_pairs={{0,4},{4,8},{8,12},{12,16},{16,20},{20,24},{24,28},{28,32},{32,36}... | collective-permute-start | bytes 196616 | tf_op jit(solution)/shard_map/ppermute | solution.py:19
  24.0 9.0 %collective-permute-start = (bf16[1,256,128]{2,1,0:T(8,128)(2,1)S(1)}, bf16[1,256,128]{2,1,0:T(8,128)(2,1)S(1)}, u32[]{:S(2)}, u32[]{:S(2)}) collective-permute-start(bf16[1,256,128]{2,1,0:T(8,128)(2,1)S(1)} %get-tuple-element.30), channel_id=1, source_target_pairs={{0,4},{4,8},{8,12},{12,16},{16,20},{20,24},{24,28},{28,32},{32,36}... | collective-permute-start | bytes 196616 | tf_op jit(solution)/shard_map/ppermute | solution.py:19
  27.6 0.7 copy-start.4
  28.3 0.7 copy-start.3
  30.3 0.9 copy-start.2
  34.0 26.0 %all-to-all-start.1 = ((bf16[128,2,128]{2,1,0:T(2,128)(2,1)}), bf16[128,2,128]{2,1,0:T(2,128)(2,1)S(1)}, u32[]{:S(2)}, u32[]{:S(2)}) async-start(bf16[128,2,128]{2,1,0:T(2,128)(2,1)} %bitcast.135), calls=%async_computation.1 | async-start | bytes 131072 | tf_op jit(solution)/shard_map/all_to_all | solution.py:122
  60.0 18.1 %all-to-all-start.2 = ((bf16[128,2,128]{2,1,0:T(2,128)(2,1)}), bf16[128,2,128]{2,1,0:T(2,128)(2,1)S(1)}, u32[]{:S(2)}, u32[]{:S(2)}) async-start(bf16[128,2,128]{2,1,0:T(2,128)(2,1)} %bitcast.133), calls=%async_computation.2 | async-start | bytes 131072 | tf_op jit(solution)/shard_map/all_to_all | solution.py:123
  66.7 59.4 %collective-permute-start.3 = (bf16[1,256,128]{1,2,0:T(8,128)(2,1)S(1)}, bf16[1,256,128]{1,2,0:T(8,128)(2,1)S(1)}, u32[]{:S(2)}, u32[]{:S(2)}) collective-permute-start(bf16[1,256,128]{1,2,0:T(8,128)(2,1)S(1)} %bitcast.167), channel_id=1, source_target_pairs={{4,0},{8,4},{12,8},{16,12},{20,16},{24,20},{28,24},{32,28},{36,32}... | collective-permute-start | bytes 196616 | tf_op jit(solution)/shard_map/ppermute | solution.py:19
  68.0 76.2 %collective-permute-start.2 = (bf16[1,256,128]{1,2,0:T(8,128)(2,1)S(1)}, bf16[1,256,128]{1,2,0:T(8,128)(2,1)S(1)}, u32[]{:S(2)}, u32[]{:S(2)}) collective-permute-start(bf16[1,256,128]{1,2,0:T(8,128)(2,1)S(1)} %bitcast.166), channel_id=1, source_target_pairs={{4,0},{8,4},{12,8},{16,12},{20,16},{24,20},{28,24},{32,28},{36,32}... | collective-permute-start | bytes 196616 | tf_op jit(solution)/shard_map/ppermute | solution.py:19
  78.1 21.5 %all-to-all-start.4 = ((bf16[128,2,128]{2,1,0:T(2,128)(2,1)}), bf16[128,2,128]{2,1,0:T(2,128)(2,1)S(1)}, u32[]{:S(2)}, u32[]{:S(2)}) async-start(bf16[128,2,128]{2,1,0:T(2,128)(2,1)} %bitcast.136), calls=%async_computation.4 | async-start | bytes 131072 | tf_op jit(solution)/shard_map/all_to_all | solution.py:148
  101.7 18.1 %all-to-all-start.3 = ((bf16[128,2,128]{2,1,0:T(2,128)(2,1)}), bf16[128,2,128]{2,1,0:T(2,128)(2,1)S(1)}, u32[]{:S(2)}, u32[]{:S(2)}) async-start(bf16[128,2,128]{2,1,0:T(2,128)(2,1)} %copy.83), calls=%async_computation.3 | async-start | bytes 131072 | tf_op jit(solution)/shard_map/all_to_all | solution.py:156
  119.8 18.3 %all-to-all-start.7 = ((bf16[128,2,128]{2,1,0:T(2,128)(2,1)}), bf16[128,2,128]{2,1,0:T(2,128)(2,1)S(1)}, u32[]{:S(2)}, u32[]{:S(2)}) async-start(bf16[128,2,128]{2,1,0:T(2,128)(2,1)} %copy.103), calls=%async_computation.7 | async-start | bytes 131072 | tf_op jit(solution)/shard_map/all_to_all | solution.py:173
  138.1 18.1 %all-to-all-start.5 = ((bf16[128,2,128]{2,1,0:T(2,128)(2,1)}), bf16[128,2,128]{2,1,0:T(2,128)(2,1)S(1)}, u32[]{:S(2)}, u32[]{:S(2)}) async-start(bf16[128,2,128]{2,1,0:T(2,128)(2,1)} %copy.93), calls=%async_computation.5 | async-start | bytes 131072 | tf_op jit(solution)/shard_map/all_to_all | solution.py:159
  156.1 18.1 %all-to-all-start.6 = ((bf16[128,2,128]{2,1,0:T(2,128)(2,1)}), bf16[128,2,128]{2,1,0:T(2,128)(2,1)S(1)}, u32[]{:S(2)}, u32[]{:S(2)}) async-start(bf16[128,2,128]{2,1,0:T(2,128)(2,1)} %copy.98), calls=%async_computation.6 | async-start | bytes 131072 | tf_op jit(solution)/shard_map/all_to_all | solution.py:166
where the time goes:
time: 176 us; the launch traced here: 175 us
  starting transfers between devices  82.4 us (47%)
  waiting for transfers between devices  71.9 us (41%)
  local copies, waits for them, and re-layouts  12.7 us (7%)
  other arithmetic  3.67 us (2%)
  matrix products  3.05 us (2%)
    all_to_all x1, starting transfers between devices, per_device(): lax.all_to_all(column_queries, 'seq', split_axis=1, concat_axis=0, tiled=...  18.4 us
    all_to_all x1, starting transfers between devices, per_device(): lax.all_to_all(column_keys, 'seq', split_axis=1, concat_axis=0, tiled=True)  14.1 us
    all_to_all x1, waiting for transfers between devices, per_device(): lax.all_to_all(column_dv.astype(jnp.bfloat16).reshape(flat_shape), 'seq',...  11.9 us
    all_to_all x1, waiting for transfers between devices, per_device(): lax.all_to_all(column_keys, 'seq', split_axis=1, concat_axis=0, tiled=True)  11.6 us
    all_to_all x1, waiting for transfers between devices, per_device(): lax.all_to_all(column_dq.astype(jnp.bfloat16).reshape(flat_shape), 'seq',...  11 us
    all_to_all x1, waiting for transfers between devices, per_device(): lax.all_to_all(column_dk.astype(jnp.bfloat16).reshape(flat_shape), 'seq',...  10.6 us
    all_to_all x1, waiting for transfers between devices, per_device(): lax.all_to_all(column_grads, 'seq', split_axis=1, concat_axis=0, tiled=True)  10.3 us
    all_to_all x1, starting transfers between devices, per_device(): lax.all_to_all(column_grads, 'seq', split_axis=1, concat_axis=0, tiled=True)  9.79 us
  transfers between devices with their start and end apart: 12, of which 7 were waited for; matrix products, arithmetic and copies ran while one was open for 9% of the time, Pallas kernels for 0%

commit v1 on v0

v1 whole, which is shorter than its diff:
```python
import jax
import jax.numpy as jnp
from jax import lax
from jax.experimental import pallas as pl
from jax.experimental.pallas import tpu as pltpu
from jax.sharding import PartitionSpec as P

MESH = pl.DeviceIdType.MESH
F32 = jnp.float32
BF16 = jnp.bfloat16
NEG = -1e30

NY = 8
NZX = 16
ROWS = NY * NZX
CW = 256
HALF = 128
DH = 64
PIECES = 4
PAIRS = PIECES // 2
BLOCK = 2 * ROWS
PART = 32
UNROLL = 7
STRIDE = 37
PACK, UNPACK, ZX_TO_Y, Y_TO_ZX, SPREAD, GATHER = range(6)


def iota(shape, axis):
    return lax.broadcasted_iota(jnp.int32, shape, axis)


def matmul(a, b):
    return lax.dot_general(a, b, (((1,), (0,)), ((), ())), preferred_element_type=F32)


def matmul_nt(a, b):
    return lax.dot_general(a, b, (((1,), (1,)), ((), ())), preferred_element_type=F32)


def matmul_tn(a, b):
    return lax.dot_general(a, b, (((0,), (0,)), ((), ())), preferred_element_type=F32)


def per_head(x):
    first = iota(x.shape, 1) < DH
    zero = jnp.zeros_like(x)
    return jnp.concatenate([jnp.where(first, x, zero), jnp.where(first, zero, x)], axis=0)


def both_heads(stacked):
    half = stacked.shape[0] // 2
    top, bottom = stacked[:half], stacked[half:]
    return jnp.where(iota(top.shape, 1) < DH, top, bottom)


def softmax(blocks):
    highest = blocks[0].max(axis=-1, keepdims=True)
    for block in blocks[1:]:
        highest = jnp.maximum(highest, block.max(axis=-1, keepdims=True))
    powers = [jnp.exp(block - highest) for block in blocks]
    total = powers[0].sum(axis=-1, keepdims=True)
    for power in powers[1:]:
        total = total + power.sum(axis=-1, keepdims=True)
    return [power / total for power in powers]


def row_attention(x_ref, kv_ref, pattern_ref, row, out_ref, total_ref):
    total_ref[...] = jnp.zeros_like(total_ref)

    @pl.loop(0, 2)
    def _(b):
        start = pl.multiple_of(b * HALF, HALF)
        rows, window = pl.ds(start, HALF), pl.ds(start, 3 * HALF)
        shape = (2 * HALF, HALF)
        same = iota(shape, 1) <= lax.rem(iota(shape, 0), HALF)
        has_earlier = jnp.broadcast_to(row >= 1, shape)
        first, second = (
            jnp.where(b == 0, pattern_ref[h, 0, 1] * jnp.minimum(row, 1), pattern_ref[h, 1, 0])
            for h in range(2)
        )
        whole_open = jnp.where(iota(shape, 0) < HALF, first, second) > 0
        q = per_head(x_ref[0, rows, :]) * jnp.asarray(0.125, BF16)
        g = per_head(x_ref[1, rows, :])
        keys, values = kv_ref[0, window, :], kv_ref[1, window, :]
        scores, weight_grads = matmul_nt(q, keys), matmul_nt(g, values)

        def chosen(x, earlier_else):
            earlier, whole, this = (x[:, i * HALF : (i + 1) * HALF] for i in range(3))
            return jnp.where(same, this, earlier_else(earlier)), whole

        diag, whole = chosen(scores, lambda x: jnp.where(has_earlier, x, NEG))
        p_diag, p_whole = softmax([diag, jnp.where(whole_open, whole, NEG)])

        def spread(at_diag, at_whole):
            at_diag, at_whole = at_diag.astype(BF16), at_whole.astype(BF16)
            zero = jnp.zeros_like(at_diag)
            return jnp.concatenate(
                [jnp.where(same, zero, at_diag), at_whole, jnp.where(same, at_diag, zero)], axis=1
            )

        w = spread(p_diag, p_whole)
        attended = both_heads(matmul(w, values)).astype(BF16)
        out_ref[0, rows, :] = attended
        wide = attended.astype(F32)
        dots = (g.astype(F32) * jnp.concatenate([wide, wide], axis=0)).sum(-1, keepdims=True)
        d_diag, d_whole = chosen(weight_grads, lambda x: x)
        e = spread(p_diag * (d_diag - dots), p_whole * (d_whole - dots))
        out_ref[1, rows, :] = (both_heads(matmul(e, keys)) * 0.125).astype(BF16)
        total_ref[0, window, :] += matmul_tn(e, q)
        total_ref[1, window, :] += matmul_tn(w, g)


def column_attention(q, k, v, g, bias):
    q = per_head(q) * jnp.asarray(0.125, BF16)
    g = per_head(g)
    (p,) = softmax([matmul_nt(q, k) + bias])
    w = p.astype(BF16)
    attended = both_heads(matmul(w, v)).astype(BF16).astype(F32)
    dots = (g.astype(F32) * jnp.concatenate([attended, attended], axis=0)).sum(-1, keepdims=True)
    e = (p * (matmul_nt(g, v) - dots)).astype(BF16)
    return attended, both_heads(matmul(e, k)) * 0.125, matmul_tn(e, q), matmul_tn(w, g)


def column_bias(pattern_ref):
    shape = (2 * ROWS, ROWS)
    stacked, key = iota(shape, 0), iota(shape, 1)
    query = lax.rem(stacked, ROWS)
    which = query // 32 + jnp.where(stacked < ROWS, 0, 4)
    bits = jnp.zeros(shape, jnp.int32)
    for h in range(2):
        for b in range(4):
            code = sum(pattern_ref[h, b, j] * (1 << j) for j in range(4))
            bits = jnp.where(which == 4 * h + b, code, bits)
    allowed = (key <= query) & (((bits >> (key // 32)) & 1) > 0)
    return jnp.where(allowed, 0.0, NEG)


def reorder(source, target):
    order, size, row = {}, 1, iota((BLOCK, BLOCK), 1)
    for name in reversed(source):
        order[name] = lax.rem(row // size, source[name])
        size *= source[name]
    place = 0
    for name in target:
        place = place * source[name] + order[name]
    return jnp.where(place == iota((BLOCK, BLOCK), 0), 1.0, 0.0).astype(BF16)


def kernel(
    q_hbm, k_hbm, v_hbm, g_hbm, row_pattern_hbm, column_pattern_hbm,
    orow, ocol,
    xc, xr, kv, back, backr, total, perm, bias,
    s1a, r1a, r1b, s2a, r2a, s2b, r2b, found, s3, r3,
    row_pattern, column_pattern, pattern_sem, in_sem, ring_sem, send_sem, recv_sem, back_send_sem, back_recv_sem,
):
    me = lax.axis_index("seq")
    y, zx = me // NZX, lax.rem(me, NZX)
    place_here = {"mp": lax.axis_index("mp"), "batch": lax.axis_index("batch")}
    after = {"seq": lax.rem(me + 1, ROWS), **place_here}
    before = {"seq": lax.rem(me + ROWS - 1, ROWS), **place_here}

    def zx_peer(i):
        other = lax.rem(zx + i, NZX)
        return other, {"seq": y * NZX + other, **place_here}

    def y_peer(i):
        other = lax.rem(y + i, NY)
        return other, {"seq": other * NZX + zx, **place_here}

    inputs = (q_hbm, k_hbm, v_hbm, g_hbm)

    this_row = pl.ds(CW, CW)
    row_places = (xr.at[0], kv.at[0, this_row], kv.at[1, this_row], xr.at[1])

    def loads_of(part, places):
        return [
            pltpu.make_async_copy(h.at[0, :, pl.ds(part * HALF, HALF)], place, in_sem.at[part, i])
            for i, (h, place) in enumerate(zip(inputs, places))
        ]

    column_loads = loads_of(1, [xc.at[i // 2, i % 2] for i in range(PIECES)])
    row_loads = loads_of(0, row_places)
    patterns = [
        pltpu.make_async_copy(row_pattern_hbm, row_pattern, pattern_sem.at[0]),
        pltpu.make_async_copy(column_pattern_hbm, column_pattern, pattern_sem.at[1]),
    ]
    for load in column_loads:
        load.start()

    barrier = pltpu.get_barrier_semaphore()

    def greet(device):
        pl.semaphore_signal(barrier, inc=1, device_id=device, device_id_type=MESH)

    @pl.loop(1, NZX, unroll=True)
    def _(i):
        greet(zx_peer(i)[1])

    @pl.loop(1, NY, unroll=True)
    def _(i):
        greet(y_peer(i)[1])

    greet(after)
    greet(before)
    for load in row_loads + patterns:
        load.start()

    def exchange(step, source, landing, over_zx):
        place = (step, 0 if over_zx else 1)
        count, peer, mine = (NZX, zx_peer, zx) if over_zx else (NY, y_peer, y)

        @pl.loop(1, count, unroll=True)
        def _(i):
            other, device = peer(i)
            pltpu.make_async_remote_copy(
                src_ref=source(other),
                dst_ref=landing(mine),
                send_sem=send_sem.at[place],
                recv_sem=recv_sem.at[place],
                device_id=device,
                device_id_type=MESH,
            ).start()

        pltpu.make_async_copy(source(mine), landing(mine), recv_sem.at[place]).start()

    def send(step, source, dest, over_zx):
        exchange(step, lambda j: source.at[:, j], lambda j: dest.at[:, j], over_zx)

    def arrived(step, whole, over_zx):
        pltpu.make_async_copy(whole, whole, recv_sem.at[step, 0 if over_zx else 1]).wait()

    def sent(step, dest, over_zx):
        part = dest.at[:, pl.ds(0, dest.shape[1] - 1)]
        pltpu.make_async_copy(part, part, send_sem.at[step, 0 if over_zx else 1]).wait()

    def last_columns(j=None):
        rows = pl.ds(HALF, HALF) if j is None else pl.ds(pl.multiple_of(HALF + j * NZX, NZX), NZX)
        return (slice(None), slice(None), rows, slice(None))

    grid_rows = {"piece": 2, "y": NY, "zx": NZX}
    by_zx = ("zx", "piece", "y")
    perm[PACK] = reorder(grid_rows, by_zx)
    for load in column_loads:
        load.wait()
    for p in range(PAIRS):
        rows = xc[p, :, :HALF, :].reshape(BLOCK, HALF)
        s1a[p] = matmul(perm[PACK], rows).astype(BF16).reshape(s1a.shape[1:])
    pl.semaphore_wait(barrier, (NZX - 1) + (NY - 1) + 2)

    send(0, s1a, r1a, True)
    exchange(0, lambda j: xc.at[last_columns(j)], lambda j: r1b.at[:, j], False)
    for load in row_loads:
        load.wait()
    forward = pltpu.make_async_remote_copy(
        src_ref=kv.at[:, this_row],
        dst_ref=kv.at[:, pl.ds(0, CW)],
        send_sem=ring_sem.at[0],
        recv_sem=ring_sem.at[1],
        device_id=after,
        device_id_type=MESH,
    )
    forward.start()

    for t, source, target in (
        (UNPACK, {"zx": NZX, "piece": 2, "y": NY}, ("piece", "y", "zx")),
        (ZX_TO_Y, {"zx": NZX, "piece": 2, "y": NY}, ("y", "piece", "zx")),
        (Y_TO_ZX, {"y": NY, "piece": 2, "zx": NZX}, ("zx", "piece", "y")),
        (SPREAD, {"piece": 2 * PIECES, "row": PART}, ("row", "piece")),
        (GATHER, {"row": PART, "piece": 2 * PIECES}, ("piece", "row")),
    ):
        perm[t] = reorder(source, target)
    for load in patterns:
        load.wait()
    bias[...] = column_bias(column_pattern)

    def swap(dest, source, t):
        for p in range(PAIRS):
            rows = source[p].reshape(BLOCK, HALF)
            dest[p] = matmul(perm[t], rows).astype(BF16).reshape(dest.shape[1:])

    arrived(0, r1a, True)
    swap(s2a, r1a, ZX_TO_Y)
    send(1, s2a, r2a, False)
    arrived(0, r1b, False)
    swap(s2b, r1b, Y_TO_ZX)
    send(1, s2b, r2b, True)

    forward.wait()
    row_attention(xr, kv, row_pattern, me, orow, total)
    back[...] = total[:, :CW, :].astype(BF16)
    backward = pltpu.make_async_remote_copy(
        src_ref=back,
        dst_ref=backr,
        send_sem=ring_sem.at[2],
        recv_sem=ring_sem.at[3],
        device_id=before,
        device_id_type=MESH,
    )
    backward.start()

    arrived(1, r2a, False)
    pieces = [r2a[i // 2, :, i % 2].reshape(ROWS, HALF) for i in range(PIECES)]
    for i, result in enumerate(column_attention(*pieces, bias[...])):
        found[0, i] = result.astype(BF16)
    arrived(1, r2b, True)
    pieces = []
    for p in range(PAIRS):
        rows = matmul(perm[UNPACK], r2b[p].reshape(BLOCK, HALF)).astype(BF16)
        pieces += [rows[:ROWS], rows[ROWS:]]
    for i, result in enumerate(column_attention(*pieces, bias[...])):
        found[1, i] = result.astype(BF16)

    for k in range(ROWS // PART):
        part = pl.ds(k * PART, PART)
        rows = found[:, :, part, :].reshape(BLOCK, HALF)
        s3[part] = matmul(perm[SPREAD], rows).astype(BF16).reshape(PART, 2 * PIECES, HALF)

    mine = back_recv_sem.at[me // PART]

    def send_back(i):
        other = lax.rem(me + i * STRIDE, ROWS)
        pltpu.make_async_remote_copy(
            src_ref=s3.at[other],
            dst_ref=r3.at[me],
            send_sem=back_send_sem,
            recv_sem=mine,
            device_id={"seq": other, **place_here},
            device_id_type=MESH,
        ).start()

    @pl.loop(0, (ROWS - 2) // UNROLL)
    def _(j):
        for u in range(UNROLL):
            send_back(1 + j * UNROLL + u)

    send_back(ROWS - 1)
    pltpu.make_async_copy(s3.at[me], r3.at[me], mine).start()

    backward.wait()
    for i in range(2):
        orow[2 + i] = (total[i, CW:, :] + backr[i].astype(F32)).astype(BF16)

    for k in range(ROWS // PART):
        part = pl.ds(k * PART, PART)
        pltpu.make_async_copy(r3.at[part], r3.at[part], back_recv_sem.at[k]).wait()
        rows = matmul(perm[GATHER], r3[part].reshape(BLOCK, HALF)).astype(BF16)
        for c in range(2):
            for i in range(PIECES):
                start = (c * PIECES + i) * PART
                ocol[i // 2, i % 2, pl.ds(c * HALF + k * PART, PART), :] = rows[start : start + PART]

    for step, (over_zx, over_y) in enumerate(((r1a, r1b), (r2b, r2a))):
        sent(step, over_zx, True)
        sent(step, over_y, False)
    others = s3.at[pl.ds(0, ROWS - 1)]
    pltpu.make_async_copy(others, others, back_send_sem).wait()


def write_out(orow, ocol, o0, o1, o2, o3, sem):
    copies = [
        pltpu.make_async_copy(ref, o.at[0, :, pl.ds(part * HALF, HALF)], sem.at[part, i])
        for i, o in enumerate((o0, o1, o2, o3))
        for part, ref in enumerate((orow.at[i], ocol.at[i // 2, i % 2]))
    ]
    for copy in copies:
        copy.start()
    for copy in copies:
        copy.wait()


def per_device(queries, key_vectors, value_vectors, cotangent, row_pattern, column_pattern):
    by_zx = pltpu.VMEM((PAIRS, NZX, 2 * NY, HALF), BF16)
    by_y = pltpu.VMEM((PAIRS, NY, 2, NZX, HALF), BF16)
    direct = pltpu.VMEM((ROWS, 2 * PIECES, HALF), BF16)
    vmem = pl.BlockSpec(memory_space=pltpu.VMEM)
    hbm = pl.BlockSpec(memory_space=pltpu.HBM)
    halves = pltpu.VMEM((PAIRS, 2, CW, HALF), BF16)
    pair = pltpu.VMEM((2, CW, HALF), BF16)
    in_hbm = [
        pltpu.with_memory_space_constraint(x, pltpu.HBM)
        for x in (queries, key_vectors, value_vectors, cotangent, row_pattern, column_pattern)
    ]
    results = pl.pallas_call(
        kernel,
        out_shape=[pltpu.VMEM((PIECES, CW, HALF), BF16), halves],
        in_specs=[hbm] * 6,
        out_specs=[vmem] * 2,
        scratch_shapes=[
            halves, pair,
            pltpu.VMEM((2, 2 * CW, HALF), BF16),
            pair, pair,
            pltpu.VMEM((2, 2 * CW, HALF), F32),
            pltpu.VMEM((6, BLOCK, BLOCK), BF16),
            pltpu.VMEM((2 * ROWS, ROWS), F32),
            by_zx, by_zx, by_y,
            by_y, by_y, by_zx, by_zx,
            pltpu.VMEM((2, PIECES, ROWS, HALF), BF16),
            direct, direct,
            pltpu.SMEM(row_pattern.shape, jnp.int32),
            pltpu.SMEM(column_pattern.shape, jnp.int32),
            pltpu.SemaphoreType.DMA((2,)),
            pltpu.SemaphoreType.DMA((2, PIECES)),
            pltpu.SemaphoreType.DMA((4,)),
            pltpu.SemaphoreType.DMA((2, 2)),
            pltpu.SemaphoreType.DMA((2, 2)),
            pltpu.SemaphoreType.DMA,
            pltpu.SemaphoreType.DMA((ROWS // PART,)),
        ],
        compiler_params=pltpu.CompilerParams(
            collective_id=0, has_side_effects=True, vmem_limit_bytes=40 * 1024 * 1024
        ),
        cost_estimate=pl.CostEstimate(
            flops=800_000_000, bytes_accessed=1_050_000, transcendentals=200_000
        ),
        name="grid_attention",
    )(*in_hbm)
    return pl.pallas_call(
        write_out,
        out_shape=[jax.ShapeDtypeStruct(queries.shape, BF16)] * 4,
        in_specs=[vmem] * 2,
        out_specs=[hbm] * 4,
        scratch_shapes=[pltpu.SemaphoreType.DMA((2, PIECES))],
        cost_estimate=pl.CostEstimate(flops=0, bytes_accessed=1_050_000, transcendentals=0),
        compiler_params=pltpu.CompilerParams(vmem_limit_bytes=8 * 1024 * 1024),
        name="write_out",
    )(*[pltpu.with_memory_space_constraint(x, pltpu.VMEM) for x in results])


def solution(mesh):
    rows = P(("batch", "seq"), None, "mp")
    heads = P("mp", None, None)
    return jax.shard_map(
        per_device,
        mesh=mesh,
        in_specs=(rows, rows, rows, rows, heads, heads),
        out_specs=(rows, rows, rows, rows),
        check_vma=False,
    )
```

time: 176 us -> 39.3 us (0.22)
  the two profiles are of different devices: /device:TPU:4 before, /device:TPU:1 now
where the time goes in v1:
time: 39.3 us; the launch traced here: 38.7 us
  Pallas kernels  38.1 us (97%)
  between operations  0.64 us (2%)
    pallas_call x1, Pallas kernels, per_device(): pl.pallas_call(kernel, out_shape=[pltpu.VMEM((PIECES, CW, HALF), BF16), h...  37.2 us
    pallas_call x1, Pallas kernels, per_device(): pl.pallas_call(write_out, out_shape=[jax.ShapeDtypeStruct(queries.shape,...  0.85 us

profile of v1, /device:TPU:1, one launch (start us, length us, event | category | flops | bytes accessed | tf_op | source)
XLA Modules:
  0.0 38.7 jit_solution(12633251751883290788)
XLA Ops:
  0.6 37.2 %grid_attention.1 = (bf16[4,256,128]{2,1,0:T(8,128)(2,1)S(1)}, bf16[2,2,256,128]{3,2,1,0:T(8,128)(2,1)S(1)}) custom-call(bf16[1,256,256]{2,1,0:T(8,128)(2,1)} %q_hbm.1, bf16[1,256,256]{2,1,0:T(8,128)(2,1)} %k_hbm.1, bf16[1,256,256]{2,1,0:T(8,128)(2,1)} %v_hbm.1, bf16[1,256,256]{2,1,0:T(8,128)(2,1)} %g_hbm.1, s32[2,2,2]{2,1,0:T(2,128)} %row_pattern_hbm.1, ...), custom_call_target="tpu_custom_call" | custom-call | flops 800000000 | bytes 1050000 | tf_op jit(solution)/shard_map/grid_attention/pallas_call | solution.py:383
  37.8 0.9 %write_out.1 = (bf16[1,256,256]{2,1,0:T(8,128)(2,1)}, bf16[1,256,256]{2,1,0:T(8,128)(2,1)}, bf16[1,256,256]{2,1,0:T(8,128)(2,1)}, bf16[1,256,256]{2,1,0:T(8,128)(2,1)}) custom-call(bf16[4,256,128]{2,1,0:T(8,128)(2,1)S(1)} %get-tuple-element.6.orow, bf16[2,2,256,128]{3,2,1,0:T(8,128)(2,1)S(1)} %get-tuple-element.7.ocol), custom_call_target="tpu_custom_call" | custom-call | bytes 1050000 | tf_op jit(solution)/shard_map/write_out/pallas_call | solution.py:417

commit v2 on v1

--- a/solution.py
+++ b/solution.py
@@ -20,9 +20,20 @@
 PAIRS = PIECES // 2
 BLOCK = 2 * ROWS
 PART = 32
-UNROLL = 7
-STRIDE = 37
 PACK, UNPACK, ZX_TO_Y, Y_TO_ZX, SPREAD, GATHER = range(6)
+
+
+def hops(offset, size):
+    return min(offset, size - offset)
+
+
+def far_first(count, distance):
+    return sorted(range(1, count), key=lambda i: (-distance(i), i * 37 % count))
+
+
+Y_ORDER = far_first(NY, lambda i: hops(i, NY))
+ZX_ORDER = far_first(NZX, lambda i: hops(i // 2, NZX // 2) + i % 2)
+ALL_ORDER = far_first(ROWS, lambda i: hops(i // NZX, NY) + hops(i % NZX // 2, NZX // 2) + i % 2)
 
 
 def iota(shape, axis):
@@ -67,15 +78,14 @@
 def row_attention(x_ref, kv_ref, pattern_ref, row, out_ref, total_ref):
     total_ref[...] = jnp.zeros_like(total_ref)
 
-    @pl.loop(0, 2)
-    def _(b):
-        start = pl.multiple_of(b * HALF, HALF)
+    for b in range(2):
+        start = b * HALF
         rows, window = pl.ds(start, HALF), pl.ds(start, 3 * HALF)
         shape = (2 * HALF, HALF)
         same = iota(shape, 1) <= lax.rem(iota(shape, 0), HALF)
         has_earlier = jnp.broadcast_to(row >= 1, shape)
         first, second = (
-            jnp.where(b == 0, pattern_ref[h, 0, 1] * jnp.minimum(row, 1), pattern_ref[h, 1, 0])
+            pattern_ref[h, b, 1 - b] * jnp.minimum(row + b, 1)
             for h in range(2)
         )
         whole_open = jnp.where(iota(shape, 0) < HALF, first, second) > 0
@@ -159,13 +169,14 @@
     after = {"seq": lax.rem(me + 1, ROWS), **place_here}
     before = {"seq": lax.rem(me + ROWS - 1, ROWS), **place_here}
 
-    def zx_peer(i):
-        other = lax.rem(zx + i, NZX)
-        return other, {"seq": y * NZX + other, **place_here}
-
-    def y_peer(i):
-        other = lax.rem(y + i, NY)
-        return other, {"seq": other * NZX + zx, **place_here}
+    zx_places = [lax.rem(zx + i, NZX) for i in range(NZX)]
+    y_places = [lax.rem(y + i, NY) for i in range(NY)]
+
+    def device(seq):
+        return {"seq": seq, **place_here}
+
+    zx_peers = [(zx_places[i], device(y * NZX + zx_places[i])) for i in ZX_ORDER]
+    y_peers = [(y_places[i], device(y_places[i] * NZX + zx)) for i in Y_ORDER]
 
     inputs = (q_hbm, k_hbm, v_hbm, g_hbm)
 
@@ -189,17 +200,11 @@
 
     barrier = pltpu.get_barrier_semaphore()
 
-    def greet(device):
-        pl.semaphore_signal(barrier, inc=1, device_id=device, device_id_type=MESH)
-
-    @pl.loop(1, NZX, unroll=True)
-    def _(i):
-        greet(zx_peer(i)[1])
-
-    @pl.loop(1, NY, unroll=True)
-    def _(i):
-        greet(y_peer(i)[1])
-
+    def greet(peer):
+        pl.semaphore_signal(barrier, inc=1, device_id=peer, device_id_type=MESH)
+
+    for _, peer in zx_peers + y_peers:
+        greet(peer)
     greet(after)
     greet(before)
     for load in row_loads + patterns:
@@ -207,20 +212,16 @@
 
     def exchange(step, source, landing, over_zx):
         place = (step, 0 if over_zx else 1)
-        count, peer, mine = (NZX, zx_peer, zx) if over_zx else (NY, y_peer, y)
-
-        @pl.loop(1, count, unroll=True)
-        def _(i):
-            other, device = peer(i)
+        peers, mine = (zx_peers, zx) if over_zx else (y_peers, y)
+        for other, peer in peers:
             pltpu.make_async_remote_copy(
                 src_ref=source(other),
                 dst_ref=landing(mine),
                 send_sem=send_sem.at[place],
                 recv_sem=recv_sem.at[place],
-                device_id=device,
+                device_id=peer,
                 device_id_type=MESH,
             ).start()
-
         pltpu.make_async_copy(source(mine), landing(mine), recv_sem.at[place]).start()
 
     def send(step, source, dest, over_zx):
@@ -315,34 +316,25 @@
         rows = found[:, :, part, :].reshape(BLOCK, HALF)
         s3[part] = matmul(perm[SPREAD], rows).astype(BF16).reshape(PART, 2 * PIECES, HALF)
 
-    mine = back_recv_sem.at[me // PART]
-
-    def send_back(i):
-        other = lax.rem(me + i * STRIDE, ROWS)
+    for i in ALL_ORDER:
+        other = y_places[i // NZX] * NZX + zx_places[i % NZX]
         pltpu.make_async_remote_copy(
             src_ref=s3.at[other],
             dst_ref=r3.at[me],
             send_sem=back_send_sem,
-            recv_sem=mine,
-            device_id={"seq": other, **place_here},
+            recv_sem=back_recv_sem,
+            device_id=device(other),
             device_id_type=MESH,
         ).start()
-
-    @pl.loop(0, (ROWS - 2) // UNROLL)
-    def _(j):
-        for u in range(UNROLL):
-            send_back(1 + j * UNROLL + u)
-
-    send_back(ROWS - 1)
-    pltpu.make_async_copy(s3.at[me], r3.at[me], mine).start()
+    pltpu.make_async_copy(s3.at[me], r3.at[me], back_recv_sem).start()
 
     backward.wait()
     for i in range(2):
         orow[2 + i] = (total[i, CW:, :] + backr[i].astype(F32)).astype(BF16)
 
+    pltpu.make_async_copy(r3, r3, back_recv_sem).wait()
     for k in range(ROWS // PART):
         part = pl.ds(k * PART, PART)
-        pltpu.make_async_copy(r3.at[part], r3.at[part], back_recv_sem.at[k]).wait()
         rows = matmul(perm[GATHER], r3[part].reshape(BLOCK, HALF)).astype(BF16)
         for c in range(2):
             for i in range(PIECES):
@@ -404,7 +396,7 @@
             pltpu.SemaphoreType.DMA((2, 2)),
             pltpu.SemaphoreType.DMA((2, 2)),
             pltpu.SemaphoreType.DMA,
-            pltpu.SemaphoreType.DMA((ROWS // PART,)),
+            pltpu.SemaphoreType.DMA,
         ],
         compiler_params=pltpu.CompilerParams(
             collective_id=0, has_side_effects=True, vmem_limit_bytes=40 * 1024 * 1024

time: 39.3 us -> 37.8 us (0.962)
  Pallas kernels: 38.1 us -> 36.8 us
    pallas_call x1, Pallas kernels: 37.2 us -> 35.9 us  [per_device(): pl.pallas_call(kernel, out_shape=[pltpu.VMEM((PIECES, CW, HALF), BF16), h...]
where the time goes in v2:
time: 37.8 us; the launch traced here: 37.4 us
  Pallas kernels  36.8 us (97%)
  between operations  0.64 us (2%)
    pallas_call x1, Pallas kernels, per_device(): pl.pallas_call(kernel, out_shape=[pltpu.VMEM((PIECES, CW, HALF), BF16), h...  35.9 us
    pallas_call x1, Pallas kernels, per_device(): pl.pallas_call(write_out, out_shape=[jax.ShapeDtypeStruct(queries.shape,...  0.85 us

profile of v2, /device:TPU:1, one launch (start us, length us, event | category | flops | bytes accessed | tf_op | source)
XLA Modules:
  0.0 37.4 jit_solution(2499158743703972946)
XLA Ops:
  0.6 35.9 %grid_attention.1 = (bf16[4,256,128]{2,1,0:T(8,128)(2,1)S(1)}, bf16[2,2,256,128]{3,2,1,0:T(8,128)(2,1)S(1)}) custom-call(bf16[1,256,256]{2,1,0:T(8,128)(2,1)} %q_hbm.1, bf16[1,256,256]{2,1,0:T(8,128)(2,1)} %k_hbm.1, bf16[1,256,256]{2,1,0:T(8,128)(2,1)} %v_hbm.1, bf16[1,256,256]{2,1,0:T(8,128)(2,1)} %g_hbm.1, s32[2,2,2]{2,1,0:T(2,128)} %row_pattern_hbm.1, ...), custom_call_target="tpu_custom_call" | custom-call | flops 800000000 | bytes 1050000 | tf_op jit(solution)/shard_map/grid_attention/pallas_call | solution.py:375
  36.6 0.9 %write_out.1 = (bf16[1,256,256]{2,1,0:T(8,128)(2,1)}, bf16[1,256,256]{2,1,0:T(8,128)(2,1)}, bf16[1,256,256]{2,1,0:T(8,128)(2,1)}, bf16[1,256,256]{2,1,0:T(8,128)(2,1)}) custom-call(bf16[4,256,128]{2,1,0:T(8,128)(2,1)S(1)} %get-tuple-element.6.orow, bf16[2,2,256,128]{3,2,1,0:T(8,128)(2,1)S(1)} %get-tuple-element.7.ocol), custom_call_target="tpu_custom_call" | custom-call | bytes 1050000 | tf_op jit(solution)/shard_map/write_out/pallas_call | solution.py:409

commit v3 on v2

--- a/solution.py
+++ b/solution.py
@@ -279,12 +279,12 @@
             rows = source[p].reshape(BLOCK, HALF)
             dest[p] = matmul(perm[t], rows).astype(BF16).reshape(dest.shape[1:])
 
+    arrived(0, r1b, False)
+    swap(s2b, r1b, Y_TO_ZX)
+    send(1, s2b, r2b, True)
     arrived(0, r1a, True)
     swap(s2a, r1a, ZX_TO_Y)
     send(1, s2a, r2a, False)
-    arrived(0, r1b, False)
-    swap(s2b, r1b, Y_TO_ZX)
-    send(1, s2b, r2b, True)
 
     forward.wait()
     row_attention(xr, kv, row_pattern, me, orow, total)
@@ -299,10 +299,6 @@
     )
     backward.start()
 
-    arrived(1, r2a, False)
-    pieces = [r2a[i // 2, :, i % 2].reshape(ROWS, HALF) for i in range(PIECES)]
-    for i, result in enumerate(column_attention(*pieces, bias[...])):
-        found[0, i] = result.astype(BF16)
     arrived(1, r2b, True)
     pieces = []
     for p in range(PAIRS):
@@ -310,6 +306,10 @@
         pieces += [rows[:ROWS], rows[ROWS:]]
     for i, result in enumerate(column_attention(*pieces, bias[...])):
         found[1, i] = result.astype(BF16)
+    arrived(1, r2a, False)
+    pieces = [r2a[i // 2, :, i % 2].reshape(ROWS, HALF) for i in range(PIECES)]
+    for i, result in enumerate(column_attention(*pieces, bias[...])):
+        found[0, i] = result.astype(BF16)
 
     for k in range(ROWS // PART):
         part = pl.ds(k * PART, PART)

time: 37.8 us -> 38.8 us (1.026)
  Pallas kernels: 36.8 us -> 37.9 us
    pallas_call x1, Pallas kernels: 35.9 us -> 37.1 us  [per_device(): pl.pallas_call(kernel, out_shape=[pltpu.VMEM((PIECES, CW, HALF), BF16), h...]
where the time goes in v3:
time: 38.8 us; the launch traced here: 38.6 us
  Pallas kernels  37.9 us (98%)
  between operations  0.64 us (2%)
    pallas_call x1, Pallas kernels, per_device(): pl.pallas_call(kernel, out_shape=[pltpu.VMEM((PIECES, CW, HALF), BF16), h...  37.1 us
    pallas_call x1, Pallas kernels, per_device(): pl.pallas_call(write_out, out_shape=[jax.ShapeDtypeStruct(queries.shape,...  0.85 us

profile of v3, /device:TPU:1, one launch (start us, length us, event | category | flops | bytes accessed | tf_op | source)
XLA Modules:
  0.0 38.6 jit_solution(4688969715386279964)
XLA Ops:
  0.6 37.1 %grid_attention.1 = (bf16[4,256,128]{2,1,0:T(8,128)(2,1)S(1)}, bf16[2,2,256,128]{3,2,1,0:T(8,128)(2,1)S(1)}) custom-call(bf16[1,256,256]{2,1,0:T(8,128)(2,1)} %q_hbm.1, bf16[1,256,256]{2,1,0:T(8,128)(2,1)} %k_hbm.1, bf16[1,256,256]{2,1,0:T(8,128)(2,1)} %v_hbm.1, bf16[1,256,256]{2,1,0:T(8,128)(2,1)} %g_hbm.1, s32[2,2,2]{2,1,0:T(2,128)} %row_pattern_hbm.1, ...), custom_call_target="tpu_custom_call" | custom-call | flops 800000000 | bytes 1050000 | tf_op jit(solution)/shard_map/grid_attention/pallas_call | solution.py:375
  37.7 0.9 %write_out.1 = (bf16[1,256,256]{2,1,0:T(8,128)(2,1)}, bf16[1,256,256]{2,1,0:T(8,128)(2,1)}, bf16[1,256,256]{2,1,0:T(8,128)(2,1)}, bf16[1,256,256]{2,1,0:T(8,128)(2,1)}) custom-call(bf16[4,256,128]{2,1,0:T(8,128)(2,1)S(1)} %get-tuple-element.6.orow, bf16[2,2,256,128]{3,2,1,0:T(8,128)(2,1)S(1)} %get-tuple-element.7.ocol), custom_call_target="tpu_custom_call" | custom-call | bytes 1050000 | tf_op jit(solution)/shard_map/write_out/pallas_call | solution.py:409

commit v4 on v2

--- a/solution.py
+++ b/solution.py
@@ -72,7 +72,8 @@
     total = powers[0].sum(axis=-1, keepdims=True)
     for power in powers[1:]:
         total = total + power.sum(axis=-1, keepdims=True)
-    return [power / total for power in powers]
+    share = 1.0 / total
+    return [power * share for power in powers]
 
 
 def row_attention(x_ref, kv_ref, pattern_ref, row, out_ref, total_ref):
@@ -110,12 +111,12 @@
 
         w = spread(p_diag, p_whole)
         attended = both_heads(matmul(w, values)).astype(BF16)
-        out_ref[0, rows, :] = attended
+        out_ref[0, rows, :HALF] = attended
         wide = attended.astype(F32)
         dots = (g.astype(F32) * jnp.concatenate([wide, wide], axis=0)).sum(-1, keepdims=True)
         d_diag, d_whole = chosen(weight_grads, lambda x: x)
         e = spread(p_diag * (d_diag - dots), p_whole * (d_whole - dots))
-        out_ref[1, rows, :] = (both_heads(matmul(e, keys)) * 0.125).astype(BF16)
+        out_ref[1, rows, :HALF] = (both_heads(matmul(e, keys)) * 0.125).astype(BF16)
         total_ref[0, window, :] += matmul_tn(e, q)
         total_ref[1, window, :] += matmul_tn(w, g)
 
@@ -158,7 +159,7 @@
 
 def kernel(
     q_hbm, k_hbm, v_hbm, g_hbm, row_pattern_hbm, column_pattern_hbm,
-    orow, ocol,
+    result,
     xc, xr, kv, back, backr, total, perm, bias,
     s1a, r1a, r1b, s2a, r2a, s2b, r2b, found, s3, r3,
     row_pattern, column_pattern, pattern_sem, in_sem, ring_sem, send_sem, recv_sem, back_send_sem, back_recv_sem,
@@ -225,13 +226,13 @@
         pltpu.make_async_copy(source(mine), landing(mine), recv_sem.at[place]).start()
 
     def send(step, source, dest, over_zx):
-        exchange(step, lambda j: source.at[:, j], lambda j: dest.at[:, j], over_zx)
+        exchange(step, lambda j: source.at[j], lambda j: dest.at[j], over_zx)
 
     def arrived(step, whole, over_zx):
         pltpu.make_async_copy(whole, whole, recv_sem.at[step, 0 if over_zx else 1]).wait()
 
     def sent(step, dest, over_zx):
-        part = dest.at[:, pl.ds(0, dest.shape[1] - 1)]
+        part = dest.at[pl.ds(0, dest.shape[0] - 1)]
         pltpu.make_async_copy(part, part, send_sem.at[step, 0 if over_zx else 1]).wait()
 
     def last_columns(j=None):
@@ -245,11 +246,12 @@
         load.wait()
     for p in range(PAIRS):
         rows = xc[p, :, :HALF, :].reshape(BLOCK, HALF)
-        s1a[p] = matmul(perm[PACK], rows).astype(BF16).reshape(s1a.shape[1:])
+        packed = matmul(perm[PACK], rows).astype(BF16)
+        s1a[:, p] = packed.reshape(NZX, 2 * NY, HALF)
     pl.semaphore_wait(barrier, (NZX - 1) + (NY - 1) + 2)
 
     send(0, s1a, r1a, True)
-    exchange(0, lambda j: xc.at[last_columns(j)], lambda j: r1b.at[:, j], False)
+    exchange(0, lambda j: xc.at[last_columns(j)], lambda j: r1b.at[j], False)
     for load in row_loads:
         load.wait()
     forward = pltpu.make_async_remote_copy(
@@ -276,8 +278,8 @@
 
     def swap(dest, source, t):
         for p in range(PAIRS):
-            rows = source[p].reshape(BLOCK, HALF)
-            dest[p] = matmul(perm[t], rows).astype(BF16).reshape(dest.shape[1:])
+            rows = matmul(perm[t], source[:, p].reshape(BLOCK, HALF)).astype(BF16)
+            dest[:, p] = rows.reshape(dest.shape[:1] + dest.shape[2:])
 
     arrived(0, r1a, True)
     swap(s2a, r1a, ZX_TO_Y)
@@ -287,7 +289,7 @@
     send(1, s2b, r2b, True)
 
     forward.wait()
-    row_attention(xr, kv, row_pattern, me, orow, total)
+    row_attention(xr, kv, row_pattern, me, result, total)
     back[...] = total[:, :CW, :].astype(BF16)
     backward = pltpu.make_async_remote_copy(
         src_ref=back,
@@ -300,16 +302,16 @@
     backward.start()
 
     arrived(1, r2a, False)
-    pieces = [r2a[i // 2, :, i % 2].reshape(ROWS, HALF) for i in range(PIECES)]
-    for i, result in enumerate(column_attention(*pieces, bias[...])):
-        found[0, i] = result.astype(BF16)
+    pieces = [r2a[:, i // 2, i % 2].reshape(ROWS, HALF) for i in range(PIECES)]
+    for i, found_here in enumerate(column_attention(*pieces, bias[...])):
+        found[0, i] = found_here.astype(BF16)
     arrived(1, r2b, True)
     pieces = []
     for p in range(PAIRS):
-        rows = matmul(perm[UNPACK], r2b[p].reshape(BLOCK, HALF)).astype(BF16)
+        rows = matmul(perm[UNPACK], r2b[:, p].reshape(BLOCK, HALF)).astype(BF16)
         pieces += [rows[:ROWS], rows[ROWS:]]
-    for i, result in enumerate(column_attention(*pieces, bias[...])):
-        found[1, i] = result.astype(BF16)
+    for i, found_here in enumerate(column_attention(*pieces, bias[...])):
+        found[1, i] = found_here.astype(BF16)
 
     for k in range(ROWS // PART):
         part = pl.ds(k * PART, PART)
@@ -330,7 +332,7 @@
 
     backward.wait()
     for i in range(2):
-        orow[2 + i] = (total[i, CW:, :] + backr[i].astype(F32)).astype(BF16)
+        result[2 + i, :, :HALF] = (total[i, CW:, :] + backr[i].astype(F32)).astype(BF16)
 
     pltpu.make_async_copy(r3, r3, back_recv_sem).wait()
     for k in range(ROWS // PART):
@@ -339,7 +341,8 @@
         for c in range(2):
             for i in range(PIECES):
                 start = (c * PIECES + i) * PART
-                ocol[i // 2, i % 2, pl.ds(c * HALF + k * PART, PART), :] = rows[start : start + PART]
+                place = pl.ds(c * HALF + k * PART, PART)
+                result[i, place, HALF:] = rows[start : start + PART]
 
     for step, (over_zx, over_y) in enumerate(((r1a, r1b), (r2b, r2a))):
         sent(step, over_zx, True)
@@ -348,11 +351,10 @@
     pltpu.make_async_copy(others, others, back_send_sem).wait()
 
 
-def write_out(orow, ocol, o0, o1, o2, o3, sem):
+def write_out(result, o0, o1, o2, o3, sem):
     copies = [
-        pltpu.make_async_copy(ref, o.at[0, :, pl.ds(part * HALF, HALF)], sem.at[part, i])
+        pltpu.make_async_copy(result.at[i], o.at[0], sem.at[i])
         for i, o in enumerate((o0, o1, o2, o3))
-        for part, ref in enumerate((orow.at[i], ocol.at[i // 2, i % 2]))
     ]
     for copy in copies:
         copy.start()
@@ -361,8 +363,8 @@
 
 
 def per_device(queries, key_vectors, value_vectors, cotangent, row_pattern, column_pattern):
-    by_zx = pltpu.VMEM((PAIRS, NZX, 2 * NY, HALF), BF16)
-    by_y = pltpu.VMEM((PAIRS, NY, 2, NZX, HALF), BF16)
+    by_zx = pltpu.VMEM((NZX, PAIRS, 2 * NY, HALF), BF16)
+    by_y = pltpu.VMEM((NY, PAIRS, 2, NZX, HALF), BF16)
     direct = pltpu.VMEM((ROWS, 2 * PIECES, HALF), BF16)
     vmem = pl.BlockSpec(memory_space=pltpu.VMEM)
     hbm = pl.BlockSpec(memory_space=pltpu.HBM)
@@ -372,11 +374,11 @@
         pltpu.with_memory_space_constraint(x, pltpu.HBM)
         for x in (queries, key_vectors, value_vectors, cotangent, row_pattern, column_pattern)
     ]
-    results = pl.pallas_call(
+    result = pl.pallas_call(
         kernel,
-        out_shape=[pltpu.VMEM((PIECES, CW, HALF), BF16), halves],
+        out_shape=pltpu.VMEM((PIECES, CW, 2 * HALF), BF16),
         in_specs=[hbm] * 6,
-        out_specs=[vmem] * 2,
+        out_specs=vmem,
         scratch_shapes=[
             halves, pair,
             pltpu.VMEM((2, 2 * CW, HALF), BF16),
@@ -409,13 +411,13 @@
     return pl.pallas_call(
         write_out,
         out_shape=[jax.ShapeDtypeStruct(queries.shape, BF16)] * 4,
-        in_specs=[vmem] * 2,
+        in_specs=[vmem],
         out_specs=[hbm] * 4,
-        scratch_shapes=[pltpu.SemaphoreType.DMA((2, PIECES))],
+        scratch_shapes=[pltpu.SemaphoreType.DMA((PIECES,))],
         cost_estimate=pl.CostEstimate(flops=0, bytes_accessed=1_050_000, transcendentals=0),
         compiler_params=pltpu.CompilerParams(vmem_limit_bytes=8 * 1024 * 1024),
         name="write_out",
-    )(*[pltpu.with_memory_space_constraint(x, pltpu.VMEM) for x in results])
+    )(pltpu.with_memory_space_constraint(result, pltpu.VMEM))
 
 
 def solution(mesh):

time: 37.8 us -> 37.8 us (level)
  no operation moved by 1% of the time
where the time goes in v4:
time: 37.8 us; the launch traced here: 37.4 us
  Pallas kernels  36.8 us (97%)
  between operations  0.64 us (2%)
    pallas_call x1, Pallas kernels, per_device(): pl.pallas_call(kernel, out_shape=pltpu.VMEM((PIECES, CW, 2 * HALF), BF16)...  35.9 us
    pallas_call x1, Pallas kernels, per_device(): pl.pallas_call(write_out, out_shape=[jax.ShapeDtypeStruct(queries.shape,...  0.82 us

profile of v4, /device:TPU:1, one launch (start us, length us, event | category | flops | bytes accessed | tf_op | source)
XLA Modules:
  0.0 37.4 jit_solution(18341594800444033193)
XLA Ops:
  0.6 35.9 %grid_attention.1.result = bf16[4,256,256]{2,1,0:T(8,128)(2,1)S(1)} custom-call(bf16[1,256,256]{2,1,0:T(8,128)(2,1)} %q_hbm.1, bf16[1,256,256]{2,1,0:T(8,128)(2,1)} %k_hbm.1, bf16[1,256,256]{2,1,0:T(8,128)(2,1)} %v_hbm.1, bf16[1,256,256]{2,1,0:T(8,128)(2,1)} %g_hbm.1, s32[2,2,2]{2,1,0:T(2,128)} %row_pattern_hbm.1, s32[2,4,4]{2,1,0:T(4,128)} %column_pattern_hbm.1), custom_call_target="tpu_custom_call" | custom-call | flops 800000000 | bytes 1050000 | tf_op jit(solution)/shard_map/grid_attention/pallas_call | solution.py:377
  36.6 0.8 %write_out.1 = (bf16[1,256,256]{2,1,0:T(8,128)(2,1)}, bf16[1,256,256]{2,1,0:T(8,128)(2,1)}, bf16[1,256,256]{2,1,0:T(8,128)(2,1)}, bf16[1,256,256]{2,1,0:T(8,128)(2,1)}) custom-call(bf16[4,256,256]{2,1,0:T(8,128)(2,1)S(1)} %grid_attention.1.result), custom_call_target="tpu_custom_call" | custom-call | bytes 1050000 | tf_op jit(solution)/shard_map/write_out/pallas_call | solution.py:411

commit v5 on v4

--- a/solution.py
+++ b/solution.py
@@ -170,8 +170,9 @@
     after = {"seq": lax.rem(me + 1, ROWS), **place_here}
     before = {"seq": lax.rem(me + ROWS - 1, ROWS), **place_here}
 
-    zx_places = [lax.rem(zx + i, NZX) for i in range(NZX)]
-    y_places = [lax.rem(y + i, NY) for i in range(NY)]
+    turn = 1 - 2 * lax.axis_index("batch")
+    zx_places = [lax.rem(zx + NZX + turn * i, NZX) for i in range(NZX)]
+    y_places = [lax.rem(y + NY + turn * i, NY) for i in range(NY)]
 
     def device(seq):
         return {"seq": seq, **place_here}
@@ -184,19 +185,26 @@
     this_row = pl.ds(CW, CW)
     row_places = (xr.at[0], kv.at[0, this_row], kv.at[1, this_row], xr.at[1])
 
-    def loads_of(part, places):
-        return [
-            pltpu.make_async_copy(h.at[0, :, pl.ds(part * HALF, HALF)], place, in_sem.at[part, i])
-            for i, (h, place) in enumerate(zip(inputs, places))
+    row_loads = [
+        pltpu.make_async_copy(h.at[0, :, pl.ds(0, HALF)], place, in_sem.at[0, i])
+        for i, (h, place) in enumerate(zip(inputs, row_places))
+    ]
+    first_loads, last_loads = (
+        [
+            pltpu.make_async_copy(
+                h.at[0, pl.ds(start, HALF), pl.ds(HALF, HALF)],
+                xc.at[i // 2, i % 2, pl.ds(start, HALF), :],
+                in_sem.at[1 + start // HALF, i],
+            )
+            for i, h in enumerate(inputs)
         ]
-
-    column_loads = loads_of(1, [xc.at[i // 2, i % 2] for i in range(PIECES)])
-    row_loads = loads_of(0, row_places)
+        for start in (0, HALF)
+    )
     patterns = [
         pltpu.make_async_copy(row_pattern_hbm, row_pattern, pattern_sem.at[0]),
         pltpu.make_async_copy(column_pattern_hbm, column_pattern, pattern_sem.at[1]),
     ]
-    for load in column_loads:
+    for load in first_loads + last_loads:
         load.start()
 
     barrier = pltpu.get_barrier_semaphore()
@@ -242,7 +250,7 @@
     grid_rows = {"piece": 2, "y": NY, "zx": NZX}
     by_zx = ("zx", "piece", "y")
     perm[PACK] = reorder(grid_rows, by_zx)
-    for load in column_loads:
+    for load in first_loads:
         load.wait()
     for p in range(PAIRS):
         rows = xc[p, :, :HALF, :].reshape(BLOCK, HALF)
@@ -251,6 +259,8 @@
     pl.semaphore_wait(barrier, (NZX - 1) + (NY - 1) + 2)
 
     send(0, s1a, r1a, True)
+    for load in last_loads:
+        load.wait()
     exchange(0, lambda j: xc.at[last_columns(j)], lambda j: r1b.at[j], False)
     for load in row_loads:
         load.wait()
@@ -393,7 +403,7 @@
             pltpu.SMEM(row_pattern.shape, jnp.int32),
             pltpu.SMEM(column_pattern.shape, jnp.int32),
             pltpu.SemaphoreType.DMA((2,)),
-            pltpu.SemaphoreType.DMA((2, PIECES)),
+            pltpu.SemaphoreType.DMA((3, PIECES)),
             pltpu.SemaphoreType.DMA((4,)),
             pltpu.SemaphoreType.DMA((2, 2)),
             pltpu.SemaphoreType.DMA((2, 2)),

time: 37.8 us -> 37.8 us (level)
  no operation moved by 1% of the time
where the time goes in v5:
time: 37.8 us; the launch traced here: 37.6 us
  Pallas kernels  36.9 us (98%)
  between operations  0.64 us (2%)
    pallas_call x1, Pallas kernels, per_device(): pl.pallas_call(kernel, out_shape=pltpu.VMEM((PIECES, CW, 2 * HALF), BF16)...  36.1 us
    pallas_call x1, Pallas kernels, per_device(): pl.pallas_call(write_out, out_shape=[jax.ShapeDtypeStruct(queries.shape,...  0.82 us

profile of v5, /device:TPU:1, one launch (start us, length us, event | category | flops | bytes accessed | tf_op | source)
XLA Modules:
  0.0 37.6 jit_solution(13288582528820172571)
XLA Ops:
  0.6 36.1 %grid_attention.1.result = bf16[4,256,256]{2,1,0:T(8,128)(2,1)S(1)} custom-call(bf16[1,256,256]{2,1,0:T(8,128)(2,1)} %q_hbm.1, bf16[1,256,256]{2,1,0:T(8,128)(2,1)} %k_hbm.1, bf16[1,256,256]{2,1,0:T(8,128)(2,1)} %v_hbm.1, bf16[1,256,256]{2,1,0:T(8,128)(2,1)} %g_hbm.1, s32[2,2,2]{2,1,0:T(2,128)} %row_pattern_hbm.1, s32[2,4,4]{2,1,0:T(4,128)} %column_pattern_hbm.1), custom_call_target="tpu_custom_call" | custom-call | flops 800000000 | bytes 1050000 | tf_op jit(solution)/shard_map/grid_attention/pallas_call | solution.py:387
  36.8 0.8 %write_out.1 = (bf16[1,256,256]{2,1,0:T(8,128)(2,1)}, bf16[1,256,256]{2,1,0:T(8,128)(2,1)}, bf16[1,256,256]{2,1,0:T(8,128)(2,1)}, bf16[1,256,256]{2,1,0:T(8,128)(2,1)}) custom-call(bf16[4,256,256]{2,1,0:T(8,128)(2,1)S(1)} %grid_attention.1.result), custom_call_target="tpu_custom_call" | custom-call | bytes 1050000 | tf_op jit(solution)/shard_map/write_out/pallas_call | solution.py:421

commit v6 on v4

--- a/solution.py
+++ b/solution.py
@@ -48,55 +48,53 @@
     return lax.dot_general(a, b, (((1,), (1,)), ((), ())), preferred_element_type=F32)
 
 
-def matmul_tn(a, b):
-    return lax.dot_general(a, b, (((0,), (0,)), ((), ())), preferred_element_type=F32)
-
-
 def per_head(x):
     first = iota(x.shape, 1) < DH
     zero = jnp.zeros_like(x)
     return jnp.concatenate([jnp.where(first, x, zero), jnp.where(first, zero, x)], axis=0)
 
 
-def both_heads(stacked):
-    half = stacked.shape[0] // 2
-    top, bottom = stacked[:half], stacked[half:]
-    return jnp.where(iota(top.shape, 1) < DH, top, bottom)
+def both_heads(wide):
+    first = iota((HALF, HALF), 0) < DH
+    return jnp.where(first, wide[:, :HALF], wide[:, HALF:])
+
+
+def head_sums(x):
+    return jnp.concatenate(
+        [x[:DH].sum(0, keepdims=True), x[DH:].sum(0, keepdims=True)], axis=1
+    )
 
 
 def softmax(blocks):
-    highest = blocks[0].max(axis=-1, keepdims=True)
+    highest = blocks[0].max(axis=0, keepdims=True)
     for block in blocks[1:]:
-        highest = jnp.maximum(highest, block.max(axis=-1, keepdims=True))
+        highest = jnp.maximum(highest, block.max(axis=0, keepdims=True))
     powers = [jnp.exp(block - highest) for block in blocks]
-    total = powers[0].sum(axis=-1, keepdims=True)
+    total = powers[0].sum(axis=0, keepdims=True)
     for power in powers[1:]:
-        total = total + power.sum(axis=-1, keepdims=True)
+        total = total + power.sum(axis=0, keepdims=True)
     share = 1.0 / total
     return [power * share for power in powers]
 
 
 def row_attention(x_ref, kv_ref, pattern_ref, row, out_ref, total_ref):
     total_ref[...] = jnp.zeros_like(total_ref)
-
+    shape = (HALF, 2 * HALF)
+    same = iota(shape, 0) <= lax.rem(iota(shape, 1), HALF)
+    has_earlier = jnp.broadcast_to(row >= 1, shape)
+    keys_t, values_t = kv_ref[0].T, kv_ref[1].T
     for b in range(2):
         start = b * HALF
         rows, window = pl.ds(start, HALF), pl.ds(start, 3 * HALF)
-        shape = (2 * HALF, HALF)
-        same = iota(shape, 1) <= lax.rem(iota(shape, 0), HALF)
-        has_earlier = jnp.broadcast_to(row >= 1, shape)
-        first, second = (
-            pattern_ref[h, b, 1 - b] * jnp.minimum(row + b, 1)
-            for h in range(2)
-        )
-        whole_open = jnp.where(iota(shape, 0) < HALF, first, second) > 0
+        first, second = (pattern_ref[h, b, 1 - b] * jnp.minimum(row + b, 1) for h in range(2))
+        whole_open = jnp.where(iota(shape, 1) < HALF, first, second) > 0
         q = per_head(x_ref[0, rows, :]) * jnp.asarray(0.125, BF16)
         g = per_head(x_ref[1, rows, :])
         keys, values = kv_ref[0, window, :], kv_ref[1, window, :]
-        scores, weight_grads = matmul_nt(q, keys), matmul_nt(g, values)
+        scores, weight_grads = matmul_nt(keys, q), matmul_nt(values, g)
 
         def chosen(x, earlier_else):
-            earlier, whole, this = (x[:, i * HALF : (i + 1) * HALF] for i in range(3))
+            earlier, whole, this = (x[i * HALF : (i + 1) * HALF] for i in range(3))
             return jnp.where(same, this, earlier_else(earlier)), whole
 
         diag, whole = chosen(scores, lambda x: jnp.where(has_earlier, x, NEG))
@@ -106,35 +104,37 @@
             at_diag, at_whole = at_diag.astype(BF16), at_whole.astype(BF16)
             zero = jnp.zeros_like(at_diag)
             return jnp.concatenate(
-                [jnp.where(same, zero, at_diag), at_whole, jnp.where(same, at_diag, zero)], axis=1
+                [jnp.where(same, zero, at_diag), at_whole, jnp.where(same, at_diag, zero)], axis=0
             )
 
         w = spread(p_diag, p_whole)
-        attended = both_heads(matmul(w, values)).astype(BF16)
-        out_ref[0, rows, :HALF] = attended
-        wide = attended.astype(F32)
-        dots = (g.astype(F32) * jnp.concatenate([wide, wide], axis=0)).sum(-1, keepdims=True)
+        attended = both_heads(matmul(values_t[:, start : start + 3 * HALF], w)).astype(BF16)
+        out_ref[0, rows, :HALF] = attended.T
+        dots = head_sums(x_ref[1, rows, :].T.astype(F32) * attended.astype(F32))
         d_diag, d_whole = chosen(weight_grads, lambda x: x)
         e = spread(p_diag * (d_diag - dots), p_whole * (d_whole - dots))
-        out_ref[1, rows, :HALF] = (both_heads(matmul(e, keys)) * 0.125).astype(BF16)
-        total_ref[0, window, :] += matmul_tn(e, q)
-        total_ref[1, window, :] += matmul_tn(w, g)
+        grad = both_heads(matmul(keys_t[:, start : start + 3 * HALF], e)) * 0.125
+        out_ref[1, rows, :HALF] = grad.astype(BF16).T
+        total_ref[0, window, :] += matmul(e, q)
+        total_ref[1, window, :] += matmul(w, g)
 
 
 def column_attention(q, k, v, g, bias):
+    g_t = g.T.astype(F32)
     q = per_head(q) * jnp.asarray(0.125, BF16)
     g = per_head(g)
-    (p,) = softmax([matmul_nt(q, k) + bias])
+    (p,) = softmax([matmul_nt(k, q) + bias])
     w = p.astype(BF16)
-    attended = both_heads(matmul(w, v)).astype(BF16).astype(F32)
-    dots = (g.astype(F32) * jnp.concatenate([attended, attended], axis=0)).sum(-1, keepdims=True)
-    e = (p * (matmul_nt(g, v) - dots)).astype(BF16)
-    return attended, both_heads(matmul(e, k)) * 0.125, matmul_tn(e, q), matmul_tn(w, g)
+    attended = both_heads(matmul(v.T, w)).astype(BF16)
+    dots = head_sums(g_t * attended.astype(F32))
+    e = (p * (matmul_nt(v, g) - dots)).astype(BF16)
+    grad = (both_heads(matmul(k.T, e)) * 0.125).astype(BF16)
+    return attended.T, grad.T, matmul(e, q).astype(BF16), matmul(w, g).astype(BF16)
 
 
 def column_bias(pattern_ref):
-    shape = (2 * ROWS, ROWS)
-    stacked, key = iota(shape, 0), iota(shape, 1)
+    shape = (ROWS, 2 * ROWS)
+    key, stacked = iota(shape, 0), iota(shape, 1)
     query = lax.rem(stacked, ROWS)
     which = query // 32 + jnp.where(stacked < ROWS, 0, 4)
     bits = jnp.zeros(shape, jnp.int32)
@@ -304,14 +304,14 @@
     arrived(1, r2a, False)
     pieces = [r2a[:, i // 2, i % 2].reshape(ROWS, HALF) for i in range(PIECES)]
     for i, found_here in enumerate(column_attention(*pieces, bias[...])):
-        found[0, i] = found_here.astype(BF16)
+        found[0, i] = found_here
     arrived(1, r2b, True)
     pieces = []
     for p in range(PAIRS):
         rows = matmul(perm[UNPACK], r2b[:, p].reshape(BLOCK, HALF)).astype(BF16)
         pieces += [rows[:ROWS], rows[ROWS:]]
     for i, found_here in enumerate(column_attention(*pieces, bias[...])):
-        found[1, i] = found_here.astype(BF16)
+        found[1, i] = found_here
 
     for k in range(ROWS // PART):
         part = pl.ds(k * PART, PART)
@@ -385,7 +385,7 @@
             pair, pair,
             pltpu.VMEM((2, 2 * CW, HALF), F32),
             pltpu.VMEM((6, BLOCK, BLOCK), BF16),
-            pltpu.VMEM((2 * ROWS, ROWS), F32),
+            pltpu.VMEM((ROWS, 2 * ROWS), F32),
             by_zx, by_zx, by_y,
             by_y, by_y, by_zx, by_zx,
             pltpu.VMEM((2, PIECES, ROWS, HALF), BF16),

time: 37.8 us -> 37.7 us (level)
  no operation moved by 1% of the time
where the time goes in v6:
time: 37.7 us; the launch traced here: 37.2 us
  Pallas kernels  36.6 us (97%)
  between operations  0.64 us (2%)
    pallas_call x1, Pallas kernels, per_device(): pl.pallas_call(kernel, out_shape=pltpu.VMEM((PIECES, CW, 2 * HALF), BF16)...  35.8 us
    pallas_call x1, Pallas kernels, per_device(): pl.pallas_call(write_out, out_shape=[jax.ShapeDtypeStruct(queries.shape,...  0.82 us

profile of v6, /device:TPU:1, one launch (start us, length us, event | category | flops | bytes accessed | tf_op | source)
XLA Modules:
  0.0 37.2 jit_solution(180677466172676054)
XLA Ops:
  0.6 35.8 %grid_attention.1.result = bf16[4,256,256]{2,1,0:T(8,128)(2,1)S(1)} custom-call(bf16[1,256,256]{2,1,0:T(8,128)(2,1)} %q_hbm.1, bf16[1,256,256]{2,1,0:T(8,128)(2,1)} %k_hbm.1, bf16[1,256,256]{2,1,0:T(8,128)(2,1)} %v_hbm.1, bf16[1,256,256]{2,1,0:T(8,128)(2,1)} %g_hbm.1, s32[2,2,2]{2,1,0:T(2,128)} %row_pattern_hbm.1, s32[2,4,4]{2,1,0:T(4,128)} %column_pattern_hbm.1), custom_call_target="tpu_custom_call" | custom-call | flops 800000000 | bytes 1050000 | tf_op jit(solution)/shard_map/grid_attention/pallas_call | solution.py:377
  36.4 0.8 %write_out.1 = (bf16[1,256,256]{2,1,0:T(8,128)(2,1)}, bf16[1,256,256]{2,1,0:T(8,128)(2,1)}, bf16[1,256,256]{2,1,0:T(8,128)(2,1)}, bf16[1,256,256]{2,1,0:T(8,128)(2,1)}) custom-call(bf16[4,256,256]{2,1,0:T(8,128)(2,1)S(1)} %grid_attention.1.result), custom_call_target="tpu_custom_call" | custom-call | bytes 1050000 | tf_op jit(solution)/shard_map/write_out/pallas_call | solution.py:411

commit v7 on v6

--- a/solution.py
+++ b/solution.py
@@ -166,7 +166,8 @@
 ):
     me = lax.axis_index("seq")
     y, zx = me // NZX, lax.rem(me, NZX)
-    place_here = {"mp": lax.axis_index("mp"), "batch": lax.axis_index("batch")}
+    batch = lax.axis_index("batch")
+    place_here = {"mp": lax.axis_index("mp"), "batch": batch}
     after = {"seq": lax.rem(me + 1, ROWS), **place_here}
     before = {"seq": lax.rem(me + ROWS - 1, ROWS), **place_here}
 
@@ -244,14 +245,18 @@
     perm[PACK] = reorder(grid_rows, by_zx)
     for load in column_loads:
         load.wait()
+    pl.semaphore_wait(barrier, (NZX - 1) + (NY - 1) + 2)
+
+    def over_y():
+        exchange(0, lambda j: xc.at[last_columns(j)], lambda j: r1b.at[j], False)
+
+    pl.when(batch == 1)(over_y)
     for p in range(PAIRS):
         rows = xc[p, :, :HALF, :].reshape(BLOCK, HALF)
         packed = matmul(perm[PACK], rows).astype(BF16)
         s1a[:, p] = packed.reshape(NZX, 2 * NY, HALF)
-    pl.semaphore_wait(barrier, (NZX - 1) + (NY - 1) + 2)
-
     send(0, s1a, r1a, True)
-    exchange(0, lambda j: xc.at[last_columns(j)], lambda j: r1b.at[j], False)
+    pl.when(batch == 0)(over_y)
     for load in row_loads:
         load.wait()
     forward = pltpu.make_async_remote_copy(

time: 37.7 us -> 38.9 us (1.032)
  the two profiles are of different devices: /device:TPU:1 before, /device:TPU:8 now
where the time goes in v7:
time: 38.9 us; the launch traced here: 38.7 us
  Pallas kernels  38.1 us (98%)
  between operations  0.64 us (2%)
    pallas_call x1, Pallas kernels, per_device(): pl.pallas_call(kernel, out_shape=pltpu.VMEM((PIECES, CW, 2 * HALF), BF16)...  37.3 us
    pallas_call x1, Pallas kernels, per_device(): pl.pallas_call(write_out, out_shape=[jax.ShapeDtypeStruct(queries.shape,...  0.82 us

profile of v7, /device:TPU:8, one launch (start us, length us, event | category | flops | bytes accessed | tf_op | source)
XLA Modules:
  0.0 38.7 jit_solution(111339245612645505)
XLA Ops:
  0.6 37.3 %grid_attention.1.result = bf16[4,256,256]{2,1,0:T(8,128)(2,1)S(1)} custom-call(bf16[1,256,256]{2,1,0:T(8,128)(2,1)} %q_hbm.1, bf16[1,256,256]{2,1,0:T(8,128)(2,1)} %k_hbm.1, bf16[1,256,256]{2,1,0:T(8,128)(2,1)} %v_hbm.1, bf16[1,256,256]{2,1,0:T(8,128)(2,1)} %g_hbm.1, s32[2,2,2]{2,1,0:T(2,128)} %row_pattern_hbm.1, s32[2,4,4]{2,1,0:T(4,128)} %column_pattern_hbm.1), custom_call_target="tpu_custom_call" | custom-call | flops 800000000 | bytes 1050000 | tf_op jit(solution)/shard_map/grid_attention/pallas_call | solution.py:382
  37.9 0.8 %write_out.1 = (bf16[1,256,256]{2,1,0:T(8,128)(2,1)}, bf16[1,256,256]{2,1,0:T(8,128)(2,1)}, bf16[1,256,256]{2,1,0:T(8,128)(2,1)}, bf16[1,256,256]{2,1,0:T(8,128)(2,1)}) custom-call(bf16[4,256,256]{2,1,0:T(8,128)(2,1)S(1)} %grid_attention.1.result), custom_call_target="tpu_custom_call" | custom-call | bytes 1050000 | tf_op jit(solution)/shard_map/write_out/pallas_call | solution.py:416

commit v8 on v6

--- a/solution.py
+++ b/solution.py
@@ -78,16 +78,15 @@
 
 
 def row_attention(x_ref, kv_ref, pattern_ref, row, out_ref, total_ref):
-    total_ref[...] = jnp.zeros_like(total_ref)
     shape = (HALF, 2 * HALF)
-    same = iota(shape, 0) <= lax.rem(iota(shape, 1), HALF)
+    same = iota(shape, 0) <= (iota((1, 2 * HALF), 1) & (HALF - 1))
     has_earlier = jnp.broadcast_to(row >= 1, shape)
     keys_t, values_t = kv_ref[0].T, kv_ref[1].T
     for b in range(2):
         start = b * HALF
         rows, window = pl.ds(start, HALF), pl.ds(start, 3 * HALF)
         first, second = (pattern_ref[h, b, 1 - b] * jnp.minimum(row + b, 1) for h in range(2))
-        whole_open = jnp.where(iota(shape, 1) < HALF, first, second) > 0
+        whole_open = jnp.where(iota((1, 2 * HALF), 1) < HALF, first, second) > 0
         q = per_head(x_ref[0, rows, :]) * jnp.asarray(0.125, BF16)
         g = per_head(x_ref[1, rows, :])
         keys, values = kv_ref[0, window, :], kv_ref[1, window, :]
@@ -115,8 +114,12 @@
         e = spread(p_diag * (d_diag - dots), p_whole * (d_whole - dots))
         grad = both_heads(matmul(keys_t[:, start : start + 3 * HALF], e)) * 0.125
         out_ref[1, rows, :HALF] = grad.astype(BF16).T
-        total_ref[0, window, :] += matmul(e, q)
-        total_ref[1, window, :] += matmul(w, g)
+        for i, term in enumerate((matmul(e, q), matmul(w, g))):
+            if b == 0:
+                total_ref[i, window, :] = term
+            else:
+                total_ref[i, HALF : 3 * HALF, :] += term[: 2 * HALF]
+                total_ref[i, 3 * HALF :, :] = term[2 * HALF :]
 
 
 def column_attention(q, k, v, g, bias):
@@ -133,23 +136,24 @@
 
 
 def column_bias(pattern_ref):
-    shape = (ROWS, 2 * ROWS)
-    key, stacked = iota(shape, 0), iota(shape, 1)
-    query = lax.rem(stacked, ROWS)
-    which = query // 32 + jnp.where(stacked < ROWS, 0, 4)
-    bits = jnp.zeros(shape, jnp.int32)
+    key, stacked = iota((ROWS, 1), 0), iota((1, 2 * ROWS), 1)
+    query = stacked & (ROWS - 1)
+    bits = jnp.zeros(stacked.shape, jnp.int32)
     for h in range(2):
         for b in range(4):
             code = sum(pattern_ref[h, b, j] * (1 << j) for j in range(4))
-            bits = jnp.where(which == 4 * h + b, code, bits)
-    allowed = (key <= query) & (((bits >> (key // 32)) & 1) > 0)
+            bits = jnp.where(stacked // 32 == 4 * h + b, code, bits)
+    seen = jnp.zeros((ROWS, 2 * ROWS), jnp.int32)
+    for j in range(4):
+        seen = jnp.where(key // 32 == j, (bits >> j) & 1, seen)
+    allowed = (key <= query) & (seen > 0)
     return jnp.where(allowed, 0.0, NEG)
 
 
 def reorder(source, target):
-    order, size, row = {}, 1, iota((BLOCK, BLOCK), 1)
+    order, size, row = {}, 1, iota((1, BLOCK), 1)
     for name in reversed(source):
-        order[name] = lax.rem(row // size, source[name])
+        order[name] = (row // size) & (source[name] - 1)
         size *= source[name]
     place = 0
     for name in target:

time: 37.7 us -> 37.7 us (level)
  no operation moved by 1% of the time
where the time goes in v8:
time: 37.7 us; the launch traced here: 37.3 us
  Pallas kernels  36.6 us (97%)
  between operations  0.64 us (2%)
    pallas_call x1, Pallas kernels, per_device(): pl.pallas_call(kernel, out_shape=pltpu.VMEM((PIECES, CW, 2 * HALF), BF16)...  35.8 us
    pallas_call x1, Pallas kernels, per_device(): pl.pallas_call(write_out, out_shape=[jax.ShapeDtypeStruct(queries.shape,...  0.82 us

profile of v8, /device:TPU:1, one launch (start us, length us, event | category | flops | bytes accessed | tf_op | source)
XLA Modules:
  0.0 37.3 jit_solution(4512771926333470103)
XLA Ops:
  0.6 35.8 %grid_attention.1.result = bf16[4,256,256]{2,1,0:T(8,128)(2,1)S(1)} custom-call(bf16[1,256,256]{2,1,0:T(8,128)(2,1)} %q_hbm.1, bf16[1,256,256]{2,1,0:T(8,128)(2,1)} %k_hbm.1, bf16[1,256,256]{2,1,0:T(8,128)(2,1)} %v_hbm.1, bf16[1,256,256]{2,1,0:T(8,128)(2,1)} %g_hbm.1, s32[2,2,2]{2,1,0:T(2,128)} %row_pattern_hbm.1, s32[2,4,4]{2,1,0:T(4,128)} %column_pattern_hbm.1), custom_call_target="tpu_custom_call" | custom-call | flops 800000000 | bytes 1050000 | tf_op jit(solution)/shard_map/grid_attention/pallas_call | solution.py:381
  36.4 0.8 %write_out.1 = (bf16[1,256,256]{2,1,0:T(8,128)(2,1)}, bf16[1,256,256]{2,1,0:T(8,128)(2,1)}, bf16[1,256,256]{2,1,0:T(8,128)(2,1)}, bf16[1,256,256]{2,1,0:T(8,128)(2,1)}) custom-call(bf16[4,256,256]{2,1,0:T(8,128)(2,1)S(1)} %grid_attention.1.result), custom_call_target="tpu_custom_call" | custom-call | bytes 1050000 | tf_op jit(solution)/shard_map/write_out/pallas_call | solution.py:415

commit v9 on v8

--- a/solution.py
+++ b/solution.py
@@ -170,7 +170,8 @@
 ):
     me = lax.axis_index("seq")
     y, zx = me // NZX, lax.rem(me, NZX)
-    place_here = {"mp": lax.axis_index("mp"), "batch": lax.axis_index("batch")}
+    batch = lax.axis_index("batch")
+    place_here = {"mp": lax.axis_index("mp"), "batch": batch}
     after = {"seq": lax.rem(me + 1, ROWS), **place_here}
     before = {"seq": lax.rem(me + ROWS - 1, ROWS), **place_here}
 
@@ -248,14 +249,18 @@
     perm[PACK] = reorder(grid_rows, by_zx)
     for load in column_loads:
         load.wait()
+    pl.semaphore_wait(barrier, (NZX - 1) + (NY - 1) + 2)
+
+    def over_y():
+        exchange(0, lambda j: xc.at[last_columns(j)], lambda j: r1b.at[j], False)
+
+    pl.when(batch == 0)(over_y)
     for p in range(PAIRS):
         rows = xc[p, :, :HALF, :].reshape(BLOCK, HALF)
         packed = matmul(perm[PACK], rows).astype(BF16)
         s1a[:, p] = packed.reshape(NZX, 2 * NY, HALF)
-    pl.semaphore_wait(barrier, (NZX - 1) + (NY - 1) + 2)
-
     send(0, s1a, r1a, True)
-    exchange(0, lambda j: xc.at[last_columns(j)], lambda j: r1b.at[j], False)
+    pl.when(batch == 1)(over_y)
     for load in row_loads:
         load.wait()
     forward = pltpu.make_async_remote_copy(

time: 37.7 us -> 38.3 us (1.016)
  Pallas kernels: 36.6 us -> 37.5 us
    pallas_call x1, Pallas kernels: 35.8 us -> 36.6 us  [per_device(): pl.pallas_call(kernel, out_shape=pltpu.VMEM((PIECES, CW, 2 * HALF), BF16)...]
where the time goes in v9:
time: 38.3 us; the launch traced here: 38.1 us
  Pallas kernels  37.5 us (98%)
  between operations  0.64 us (2%)
    pallas_call x1, Pallas kernels, per_device(): pl.pallas_call(kernel, out_shape=pltpu.VMEM((PIECES, CW, 2 * HALF), BF16)...  36.6 us
    pallas_call x1, Pallas kernels, per_device(): pl.pallas_call(write_out, out_shape=[jax.ShapeDtypeStruct(queries.shape,...  0.82 us

profile of v9, /device:TPU:1, one launch (start us, length us, event | category | flops | bytes accessed | tf_op | source)
XLA Modules:
  0.0 38.1 jit_solution(1077209271680807099)
XLA Ops:
  0.6 36.6 %grid_attention.1.result = bf16[4,256,256]{2,1,0:T(8,128)(2,1)S(1)} custom-call(bf16[1,256,256]{2,1,0:T(8,128)(2,1)} %q_hbm.1, bf16[1,256,256]{2,1,0:T(8,128)(2,1)} %k_hbm.1, bf16[1,256,256]{2,1,0:T(8,128)(2,1)} %v_hbm.1, bf16[1,256,256]{2,1,0:T(8,128)(2,1)} %g_hbm.1, s32[2,2,2]{2,1,0:T(2,128)} %row_pattern_hbm.1, s32[2,4,4]{2,1,0:T(4,128)} %column_pattern_hbm.1), custom_call_target="tpu_custom_call" | custom-call | flops 800000000 | bytes 1050000 | tf_op jit(solution)/shard_map/grid_attention/pallas_call | solution.py:386
  37.3 0.8 %write_out.1 = (bf16[1,256,256]{2,1,0:T(8,128)(2,1)}, bf16[1,256,256]{2,1,0:T(8,128)(2,1)}, bf16[1,256,256]{2,1,0:T(8,128)(2,1)}, bf16[1,256,256]{2,1,0:T(8,128)(2,1)}) custom-call(bf16[4,256,256]{2,1,0:T(8,128)(2,1)S(1)} %grid_attention.1.result), custom_call_target="tpu_custom_call" | custom-call | bytes 1050000 | tf_op jit(solution)/shard_map/write_out/pallas_call | solution.py:420

commit v10 on v8

--- a/solution.py
+++ b/solution.py
@@ -77,11 +77,11 @@
     return [power * share for power in powers]
 
 
-def row_attention(x_ref, kv_ref, pattern_ref, row, out_ref, total_ref):
+def row_attention(x_ref, kv_ref, pattern_ref, row, out_ref, total_ref, w_ref, e_ref):
     shape = (HALF, 2 * HALF)
     same = iota(shape, 0) <= (iota((1, 2 * HALF), 1) & (HALF - 1))
     has_earlier = jnp.broadcast_to(row >= 1, shape)
-    keys_t, values_t = kv_ref[0].T, kv_ref[1].T
+    values_t = kv_ref[1].T
     for b in range(2):
         start = b * HALF
         rows, window = pl.ds(start, HALF), pl.ds(start, 3 * HALF)
@@ -112,14 +112,32 @@
         dots = head_sums(x_ref[1, rows, :].T.astype(F32) * attended.astype(F32))
         d_diag, d_whole = chosen(weight_grads, lambda x: x)
         e = spread(p_diag * (d_diag - dots), p_whole * (d_whole - dots))
+        w_ref[b], e_ref[b] = w, e
+        earlier = 2 * HALF - start
+        for i, term in enumerate((matmul(e[:earlier], q), matmul(w[:earlier], g))):
+            if b == 0:
+                total_ref[i, : 2 * HALF, :] = term
+            else:
+                total_ref[i, HALF : 2 * HALF, :] += term
+
+
+def row_gradients(x_ref, kv_ref, out_ref, total_ref, w_ref, e_ref):
+    keys_t = kv_ref[0].T
+    for b in range(2):
+        start = b * HALF
+        rows = pl.ds(start, HALF)
+        q = per_head(x_ref[0, rows, :]) * jnp.asarray(0.125, BF16)
+        g = per_head(x_ref[1, rows, :])
+        w, e = w_ref[b], e_ref[b]
         grad = both_heads(matmul(keys_t[:, start : start + 3 * HALF], e)) * 0.125
         out_ref[1, rows, :HALF] = grad.astype(BF16).T
-        for i, term in enumerate((matmul(e, q), matmul(w, g))):
+        earlier = 2 * HALF - start
+        for i, term in enumerate((matmul(e[earlier:], q), matmul(w[earlier:], g))):
             if b == 0:
-                total_ref[i, window, :] = term
+                total_ref[i, 2 * HALF : 3 * HALF, :] = term
             else:
-                total_ref[i, HALF : 3 * HALF, :] += term[: 2 * HALF]
-                total_ref[i, 3 * HALF :, :] = term[2 * HALF :]
+                total_ref[i, 2 * HALF : 3 * HALF, :] += term[:HALF]
+                total_ref[i, 3 * HALF :, :] = term[HALF:]
 
 
 def column_attention(q, k, v, g, bias):
@@ -164,7 +182,7 @@
 def kernel(
     q_hbm, k_hbm, v_hbm, g_hbm, row_pattern_hbm, column_pattern_hbm,
     result,
-    xc, xr, kv, back, backr, total, perm, bias,
+    xc, xr, kv, back, backr, total, row_w, row_e, perm, bias,
     s1a, r1a, r1b, s2a, r2a, s2b, r2b, found, s3, r3,
     row_pattern, column_pattern, pattern_sem, in_sem, ring_sem, send_sem, recv_sem, back_send_sem, back_recv_sem,
 ):
@@ -293,7 +311,7 @@
     send(1, s2b, r2b, True)
 
     forward.wait()
-    row_attention(xr, kv, row_pattern, me, result, total)
+    row_attention(xr, kv, row_pattern, me, result, total, row_w, row_e)
     back[...] = total[:, :CW, :].astype(BF16)
     backward = pltpu.make_async_remote_copy(
         src_ref=back,
@@ -306,16 +324,16 @@
     backward.start()
 
     arrived(1, r2a, False)
-    pieces = [r2a[:, i // 2, i % 2].reshape(ROWS, HALF) for i in range(PIECES)]
-    for i, found_here in enumerate(column_attention(*pieces, bias[...])):
-        found[0, i] = found_here
     arrived(1, r2b, True)
-    pieces = []
+    first = [r2a[:, i // 2, i % 2].reshape(ROWS, HALF) for i in range(PIECES)]
+    second = []
     for p in range(PAIRS):
         rows = matmul(perm[UNPACK], r2b[:, p].reshape(BLOCK, HALF)).astype(BF16)
-        pieces += [rows[:ROWS], rows[ROWS:]]
-    for i, found_here in enumerate(column_attention(*pieces, bias[...])):
-        found[1, i] = found_here
+        second += [rows[:ROWS], rows[ROWS:]]
+    results = [column_attention(*pieces, bias[...]) for pieces in (first, second)]
+    for c in range(2):
+        for i in range(PIECES):
+            found[c, i] = results[c][i]
 
     for k in range(ROWS // PART):
         part = pl.ds(k * PART, PART)
@@ -334,6 +352,7 @@
         ).start()
     pltpu.make_async_copy(s3.at[me], r3.at[me], back_recv_sem).start()
 
+    row_gradients(xr, kv, result, total, row_w, row_e)
     backward.wait()
     for i in range(2):
         result[2 + i, :, :HALF] = (total[i, CW:, :] + backr[i].astype(F32)).astype(BF16)
@@ -369,6 +388,7 @@
 def per_device(queries, key_vectors, value_vectors, cotangent, row_pattern, column_pattern):
     by_zx = pltpu.VMEM((NZX, PAIRS, 2 * NY, HALF), BF16)
     by_y = pltpu.VMEM((NY, PAIRS, 2, NZX, HALF), BF16)
+    weights = pltpu.VMEM((2, 3 * HALF, 2 * HALF), BF16)
     direct = pltpu.VMEM((ROWS, 2 * PIECES, HALF), BF16)
     vmem = pl.BlockSpec(memory_space=pltpu.VMEM)
     hbm = pl.BlockSpec(memory_space=pltpu.HBM)
@@ -388,6 +408,7 @@
             pltpu.VMEM((2, 2 * CW, HALF), BF16),
             pair, pair,
             pltpu.VMEM((2, 2 * CW, HALF), F32),
+            weights, weights,
             pltpu.VMEM((6, BLOCK, BLOCK), BF16),
             pltpu.VMEM((ROWS, 2 * ROWS), F32),
             by_zx, by_zx, by_y,

time: 37.7 us -> 38.1 us (1.011)
  Pallas kernels: 36.6 us -> 37.3 us
    pallas_call x1, Pallas kernels: 35.8 us -> 36.5 us  [per_device(): pl.pallas_call(kernel, out_shape=pltpu.VMEM((PIECES, CW, 2 * HALF), BF16)...]
where the time goes in v10:
time: 38.1 us; the launch traced here: 38 us
  Pallas kernels  37.3 us (98%)
  between operations  0.64 us (2%)
    pallas_call x1, Pallas kernels, per_device(): pl.pallas_call(kernel, out_shape=pltpu.VMEM((PIECES, CW, 2 * HALF), BF16)...  36.5 us
    pallas_call x1, Pallas kernels, per_device(): pl.pallas_call(write_out, out_shape=[jax.ShapeDtypeStruct(queries.shape,...  0.82 us

profile of v10, /device:TPU:1, one launch (start us, length us, event | category | flops | bytes accessed | tf_op | source)
XLA Modules:
  0.0 38.0 jit_solution(8436446664845167982)
XLA Ops:
  0.6 36.5 %grid_attention.1.result = bf16[4,256,256]{2,1,0:T(8,128)(2,1)S(1)} custom-call(bf16[1,256,256]{2,1,0:T(8,128)(2,1)} %q_hbm.1, bf16[1,256,256]{2,1,0:T(8,128)(2,1)} %k_hbm.1, bf16[1,256,256]{2,1,0:T(8,128)(2,1)} %v_hbm.1, bf16[1,256,256]{2,1,0:T(8,128)(2,1)} %g_hbm.1, s32[2,2,2]{2,1,0:T(2,128)} %row_pattern_hbm.1, s32[2,4,4]{2,1,0:T(4,128)} %column_pattern_hbm.1), custom_call_target="tpu_custom_call" | custom-call | flops 800000000 | bytes 1050000 | tf_op jit(solution)/shard_map/grid_attention/pallas_call | solution.py:401
  37.1 0.8 %write_out.1 = (bf16[1,256,256]{2,1,0:T(8,128)(2,1)}, bf16[1,256,256]{2,1,0:T(8,128)(2,1)}, bf16[1,256,256]{2,1,0:T(8,128)(2,1)}, bf16[1,256,256]{2,1,0:T(8,128)(2,1)}) custom-call(bf16[4,256,256]{2,1,0:T(8,128)(2,1)S(1)} %grid_attention.1.result), custom_call_target="tpu_custom_call" | custom-call | bytes 1050000 | tf_op jit(solution)/shard_map/write_out/pallas_call | solution.py:436

commit v11 on v10

--- a/solution.py
+++ b/solution.py
@@ -304,10 +304,10 @@
             dest[:, p] = rows.reshape(dest.shape[:1] + dest.shape[2:])
 
     arrived(0, r1a, True)
+    arrived(0, r1b, False)
     swap(s2a, r1a, ZX_TO_Y)
+    swap(s2b, r1b, Y_TO_ZX)
     send(1, s2a, r2a, False)
-    arrived(0, r1b, False)
-    swap(s2b, r1b, Y_TO_ZX)
     send(1, s2b, r2b, True)
 
     forward.wait()
@@ -324,16 +324,16 @@
     backward.start()
 
     arrived(1, r2a, False)
+    pieces = [r2a[:, i // 2, i % 2].reshape(ROWS, HALF) for i in range(PIECES)]
+    for i, found_here in enumerate(column_attention(*pieces, bias[...])):
+        found[0, i] = found_here
     arrived(1, r2b, True)
-    first = [r2a[:, i // 2, i % 2].reshape(ROWS, HALF) for i in range(PIECES)]
-    second = []
+    pieces = []
     for p in range(PAIRS):
         rows = matmul(perm[UNPACK], r2b[:, p].reshape(BLOCK, HALF)).astype(BF16)
-        second += [rows[:ROWS], rows[ROWS:]]
-    results = [column_attention(*pieces, bias[...]) for pieces in (first, second)]
-    for c in range(2):
-        for i in range(PIECES):
-            found[c, i] = results[c][i]
+        pieces += [rows[:ROWS], rows[ROWS:]]
+    for i, found_here in enumerate(column_attention(*pieces, bias[...])):
+        found[1, i] = found_here
 
     for k in range(ROWS // PART):
         part = pl.ds(k * PART, PART)

time: 38.1 us -> 37.8 us (level)
  no operation moved by 1% of the time
where the time goes in v11:
time: 37.8 us; the launch traced here: 37.6 us
  Pallas kernels  37 us (98%)
  between operations  0.64 us (2%)
    pallas_call x1, Pallas kernels, per_device(): pl.pallas_call(kernel, out_shape=pltpu.VMEM((PIECES, CW, 2 * HALF), BF16)...  36.2 us
    pallas_call x1, Pallas kernels, per_device(): pl.pallas_call(write_out, out_shape=[jax.ShapeDtypeStruct(queries.shape,...  0.82 us

profile of v11, /device:TPU:1, one launch (start us, length us, event | category | flops | bytes accessed | tf_op | source)
XLA Modules:
  0.0 37.6 jit_solution(7182768507326095961)
XLA Ops:
  0.6 36.2 %grid_attention.1.result = bf16[4,256,256]{2,1,0:T(8,128)(2,1)S(1)} custom-call(bf16[1,256,256]{2,1,0:T(8,128)(2,1)} %q_hbm.1, bf16[1,256,256]{2,1,0:T(8,128)(2,1)} %k_hbm.1, bf16[1,256,256]{2,1,0:T(8,128)(2,1)} %v_hbm.1, bf16[1,256,256]{2,1,0:T(8,128)(2,1)} %g_hbm.1, s32[2,2,2]{2,1,0:T(2,128)} %row_pattern_hbm.1, s32[2,4,4]{2,1,0:T(4,128)} %column_pattern_hbm.1), custom_call_target="tpu_custom_call" | custom-call | flops 800000000 | bytes 1050000 | tf_op jit(solution)/shard_map/grid_attention/pallas_call | solution.py:401
  36.8 0.8 %write_out.1 = (bf16[1,256,256]{2,1,0:T(8,128)(2,1)}, bf16[1,256,256]{2,1,0:T(8,128)(2,1)}, bf16[1,256,256]{2,1,0:T(8,128)(2,1)}, bf16[1,256,256]{2,1,0:T(8,128)(2,1)}) custom-call(bf16[4,256,256]{2,1,0:T(8,128)(2,1)S(1)} %grid_attention.1.result), custom_call_target="tpu_custom_call" | custom-call | bytes 1050000 | tf_op jit(solution)/shard_map/write_out/pallas_call | solution.py:436

commit v12 on v11

--- a/solution.py
+++ b/solution.py
@@ -304,10 +304,10 @@
             dest[:, p] = rows.reshape(dest.shape[:1] + dest.shape[2:])
 
     arrived(0, r1a, True)
+    swap(s2a, r1a, ZX_TO_Y)
+    send(1, s2a, r2a, False)
     arrived(0, r1b, False)
-    swap(s2a, r1a, ZX_TO_Y)
     swap(s2b, r1b, Y_TO_ZX)
-    send(1, s2a, r2a, False)
     send(1, s2b, r2b, True)
 
     forward.wait()

time: 37.8 us -> 37.6 us (level)
  Pallas kernels: 37 us -> 36.6 us
where the time goes in v12:
time: 37.6 us; the launch traced here: 37.3 us
  Pallas kernels  36.6 us (97%)
  between operations  0.64 us (2%)
    pallas_call x1, Pallas kernels, per_device(): pl.pallas_call(kernel, out_shape=pltpu.VMEM((PIECES, CW, 2 * HALF), BF16)...  35.8 us
    pallas_call x1, Pallas kernels, per_device(): pl.pallas_call(write_out, out_shape=[jax.ShapeDtypeStruct(queries.shape,...  0.82 us

profile of v12, /device:TPU:1, one launch (start us, length us, event | category | flops | bytes accessed | tf_op | source)
XLA Modules:
  0.0 37.3 jit_solution(18438355339100404598)
XLA Ops:
  0.6 35.8 %grid_attention.1.result = bf16[4,256,256]{2,1,0:T(8,128)(2,1)S(1)} custom-call(bf16[1,256,256]{2,1,0:T(8,128)(2,1)} %q_hbm.1, bf16[1,256,256]{2,1,0:T(8,128)(2,1)} %k_hbm.1, bf16[1,256,256]{2,1,0:T(8,128)(2,1)} %v_hbm.1, bf16[1,256,256]{2,1,0:T(8,128)(2,1)} %g_hbm.1, s32[2,2,2]{2,1,0:T(2,128)} %row_pattern_hbm.1, s32[2,4,4]{2,1,0:T(4,128)} %column_pattern_hbm.1), custom_call_target="tpu_custom_call" | custom-call | flops 800000000 | bytes 1050000 | tf_op jit(solution)/shard_map/grid_attention/pallas_call | solution.py:401
  36.4 0.8 %write_out.1 = (bf16[1,256,256]{2,1,0:T(8,128)(2,1)}, bf16[1,256,256]{2,1,0:T(8,128)(2,1)}, bf16[1,256,256]{2,1,0:T(8,128)(2,1)}, bf16[1,256,256]{2,1,0:T(8,128)(2,1)}) custom-call(bf16[4,256,256]{2,1,0:T(8,128)(2,1)S(1)} %grid_attention.1.result), custom_call_target="tpu_custom_call" | custom-call | bytes 1050000 | tf_op jit(solution)/shard_map/write_out/pallas_call | solution.py:436

commit v13 on v8

--- a/solution.py
+++ b/solution.py
@@ -322,30 +322,32 @@
         rows = found[:, :, part, :].reshape(BLOCK, HALF)
         s3[part] = matmul(perm[SPREAD], rows).astype(BF16).reshape(PART, 2 * PIECES, HALF)
 
+    mine = back_recv_sem.at[me // PART]
     for i in ALL_ORDER:
         other = y_places[i // NZX] * NZX + zx_places[i % NZX]
         pltpu.make_async_remote_copy(
             src_ref=s3.at[other],
             dst_ref=r3.at[me],
             send_sem=back_send_sem,
-            recv_sem=back_recv_sem,
+            recv_sem=mine,
             device_id=device(other),
             device_id_type=MESH,
         ).start()
-    pltpu.make_async_copy(s3.at[me], r3.at[me], back_recv_sem).start()
+    pltpu.make_async_copy(s3.at[me], r3.at[me], mine).start()
 
     backward.wait()
     for i in range(2):
         result[2 + i, :, :HALF] = (total[i, CW:, :] + backr[i].astype(F32)).astype(BF16)
 
-    pltpu.make_async_copy(r3, r3, back_recv_sem).wait()
-    for k in range(ROWS // PART):
-        part = pl.ds(k * PART, PART)
+    for k in (2, 1, 3, 0):
+        k = lax.rem(me // PART + k, ROWS // PART)
+        part = pl.ds(pl.multiple_of(k * PART, PART), PART)
+        pltpu.make_async_copy(r3.at[part], r3.at[part], back_recv_sem.at[k]).wait()
         rows = matmul(perm[GATHER], r3[part].reshape(BLOCK, HALF)).astype(BF16)
         for c in range(2):
             for i in range(PIECES):
                 start = (c * PIECES + i) * PART
-                place = pl.ds(c * HALF + k * PART, PART)
+                place = pl.ds(pl.multiple_of(c * HALF + k * PART, PART), PART)
                 result[i, place, HALF:] = rows[start : start + PART]
 
     for step, (over_zx, over_y) in enumerate(((r1a, r1b), (r2b, r2a))):
@@ -402,7 +404,7 @@
             pltpu.SemaphoreType.DMA((2, 2)),
             pltpu.SemaphoreType.DMA((2, 2)),
             pltpu.SemaphoreType.DMA,
-            pltpu.SemaphoreType.DMA,
+            pltpu.SemaphoreType.DMA((ROWS // PART,)),
         ],
         compiler_params=pltpu.CompilerParams(
             collective_id=0, has_side_effects=True, vmem_limit_bytes=40 * 1024 * 1024

time: 37.7 us -> 37.6 us (level)
  no operation moved by 1% of the time
where the time goes in v13:
time: 37.6 us; the launch traced here: 37.2 us
  Pallas kernels  36.6 us (97%)
  between operations  0.64 us (2%)
    pallas_call x1, Pallas kernels, per_device(): pl.pallas_call(kernel, out_shape=pltpu.VMEM((PIECES, CW, 2 * HALF), BF16)...  35.8 us
    pallas_call x1, Pallas kernels, per_device(): pl.pallas_call(write_out, out_shape=[jax.ShapeDtypeStruct(queries.shape,...  0.82 us

profile of v13, /device:TPU:1, one launch (start us, length us, event | category | flops | bytes accessed | tf_op | source)
XLA Modules:
  0.0 37.2 jit_solution(2122996332589969317)
XLA Ops:
  0.6 35.8 %grid_attention.1.result = bf16[4,256,256]{2,1,0:T(8,128)(2,1)S(1)} custom-call(bf16[1,256,256]{2,1,0:T(8,128)(2,1)} %q_hbm.1, bf16[1,256,256]{2,1,0:T(8,128)(2,1)} %k_hbm.1, bf16[1,256,256]{2,1,0:T(8,128)(2,1)} %v_hbm.1, bf16[1,256,256]{2,1,0:T(8,128)(2,1)} %g_hbm.1, s32[2,2,2]{2,1,0:T(2,128)} %row_pattern_hbm.1, s32[2,4,4]{2,1,0:T(4,128)} %column_pattern_hbm.1), custom_call_target="tpu_custom_call" | custom-call | flops 800000000 | bytes 1050000 | tf_op jit(solution)/shard_map/grid_attention/pallas_call | solution.py:383
  36.4 0.8 %write_out.1 = (bf16[1,256,256]{2,1,0:T(8,128)(2,1)}, bf16[1,256,256]{2,1,0:T(8,128)(2,1)}, bf16[1,256,256]{2,1,0:T(8,128)(2,1)}, bf16[1,256,256]{2,1,0:T(8,128)(2,1)}) custom-call(bf16[4,256,256]{2,1,0:T(8,128)(2,1)S(1)} %grid_attention.1.result), custom_call_target="tpu_custom_call" | custom-call | bytes 1050000 | tf_op jit(solution)/shard_map/write_out/pallas_call | solution.py:417

commit v14 on v8

--- a/solution.py
+++ b/solution.py
@@ -19,6 +19,7 @@
 PIECES = 4
 PAIRS = PIECES // 2
 BLOCK = 2 * ROWS
+CHUNK = 64
 PART = 32
 PACK, UNPACK, ZX_TO_Y, Y_TO_ZX, SPREAD, GATHER = range(6)
 
@@ -258,15 +259,28 @@
     exchange(0, lambda j: xc.at[last_columns(j)], lambda j: r1b.at[j], False)
     for load in row_loads:
         load.wait()
-    forward = pltpu.make_async_remote_copy(
-        src_ref=kv.at[:, this_row],
-        dst_ref=kv.at[:, pl.ds(0, CW)],
-        send_sem=ring_sem.at[0],
-        recv_sem=ring_sem.at[1],
-        device_id=after,
-        device_id_type=MESH,
+
+    def start_pieces(source, dest, first_sem, peer):
+        for i in range(2):
+            for start in range(0, CW, CHUNK):
+                pltpu.make_async_remote_copy(
+                    src_ref=source(i, start),
+                    dst_ref=dest(i, start),
+                    send_sem=ring_sem.at[first_sem],
+                    recv_sem=ring_sem.at[first_sem + 1],
+                    device_id=peer,
+                    device_id_type=MESH,
+                ).start()
+
+    def wait_pieces(whole, sem):
+        pltpu.make_async_copy(whole, whole, ring_sem.at[sem]).wait()
+
+    start_pieces(
+        lambda i, start: kv.at[i, pl.ds(CW + start, CHUNK)],
+        lambda i, start: kv.at[i, pl.ds(start, CHUNK)],
+        0,
+        after,
     )
-    forward.start()
 
     for t, source, target in (
         (UNPACK, {"zx": NZX, "piece": 2, "y": NY}, ("piece", "y", "zx")),
@@ -292,18 +306,15 @@
     swap(s2b, r1b, Y_TO_ZX)
     send(1, s2b, r2b, True)
 
-    forward.wait()
+    wait_pieces(kv.at[:, pl.ds(0, CW)], 1)
     row_attention(xr, kv, row_pattern, me, result, total)
     back[...] = total[:, :CW, :].astype(BF16)
-    backward = pltpu.make_async_remote_copy(
-        src_ref=back,
-        dst_ref=backr,
-        send_sem=ring_sem.at[2],
-        recv_sem=ring_sem.at[3],
-        device_id=before,
-        device_id_type=MESH,
+    start_pieces(
+        lambda i, start: back.at[i, pl.ds(start, CHUNK)],
+        lambda i, start: backr.at[i, pl.ds(start, CHUNK)],
+        2,
+        before,
     )
-    backward.start()
 
     arrived(1, r2a, False)
     pieces = [r2a[:, i // 2, i % 2].reshape(ROWS, HALF) for i in range(PIECES)]
@@ -334,7 +345,7 @@
         ).start()
     pltpu.make_async_copy(s3.at[me], r3.at[me], back_recv_sem).start()
 
-    backward.wait()
+    wait_pieces(backr, 3)
     for i in range(2):
         result[2 + i, :, :HALF] = (total[i, CW:, :] + backr[i].astype(F32)).astype(BF16)
 
@@ -351,6 +362,8 @@
     for step, (over_zx, over_y) in enumerate(((r1a, r1b), (r2b, r2a))):
         sent(step, over_zx, True)
         sent(step, over_y, False)
+    wait_pieces(back, 0)
+    wait_pieces(back, 2)
     others = s3.at[pl.ds(0, ROWS - 1)]
     pltpu.make_async_copy(others, others, back_send_sem).wait()
 

time: 37.7 us -> 37.7 us (level)
  no operation moved by 1% of the time
where the time goes in v14:
time: 37.7 us; the launch traced here: 37.3 us
  Pallas kernels  36.6 us (97%)
  between operations  0.64 us (2%)
    pallas_call x1, Pallas kernels, per_device(): pl.pallas_call(kernel, out_shape=pltpu.VMEM((PIECES, CW, 2 * HALF), BF16)...  35.8 us
    pallas_call x1, Pallas kernels, per_device(): pl.pallas_call(write_out, out_shape=[jax.ShapeDtypeStruct(queries.shape,...  0.82 us

profile of v14, /device:TPU:1, one launch (start us, length us, event | category | flops | bytes accessed | tf_op | source)
XLA Modules:
  0.0 37.3 jit_solution(7388607270938554587)
XLA Ops:
  0.6 35.8 %grid_attention.1.result = bf16[4,256,256]{2,1,0:T(8,128)(2,1)S(1)} custom-call(bf16[1,256,256]{2,1,0:T(8,128)(2,1)} %q_hbm.1, bf16[1,256,256]{2,1,0:T(8,128)(2,1)} %k_hbm.1, bf16[1,256,256]{2,1,0:T(8,128)(2,1)} %v_hbm.1, bf16[1,256,256]{2,1,0:T(8,128)(2,1)} %g_hbm.1, s32[2,2,2]{2,1,0:T(2,128)} %row_pattern_hbm.1, s32[2,4,4]{2,1,0:T(4,128)} %column_pattern_hbm.1), custom_call_target="tpu_custom_call" | custom-call | flops 800000000 | bytes 1050000 | tf_op jit(solution)/shard_map/grid_attention/pallas_call | solution.py:394
  36.5 0.8 %write_out.1 = (bf16[1,256,256]{2,1,0:T(8,128)(2,1)}, bf16[1,256,256]{2,1,0:T(8,128)(2,1)}, bf16[1,256,256]{2,1,0:T(8,128)(2,1)}, bf16[1,256,256]{2,1,0:T(8,128)(2,1)}) custom-call(bf16[4,256,256]{2,1,0:T(8,128)(2,1)S(1)} %grid_attention.1.result), custom_call_target="tpu_custom_call" | custom-call | bytes 1050000 | tf_op jit(solution)/shard_map/write_out/pallas_call | solution.py:428
